TPU v7x, 32 devices: a whole 2x2x4 slice. The times are simulated.
32 devices in a mesh: row: 4 (over y, x), col: 4 (over z), depth: 2 (over core).
Axes of the slice: x: 2, y: 2, z: 4, core: 2. Of those that a mesh axis runs over, the one named last changes fastest.
Arguments:
- tokens: bfloat16 [1024, 8192], P(('col', 'depth'), 'row'), may hold values from -6 to 6
- out_grad: bfloat16 [1024, 8192], P(('col', 'depth'), 'row'), may hold values from -6 to 6
- gate_weight: bfloat16 [8192, 14336], P('row', ('col', 'depth')), may hold values from -0.0625 to 0.0625
- up_weight: bfloat16 [8192, 14336], P('row', ('col', 'depth')), may hold values from -0.0625 to 0.0625
- down_weight: bfloat16 [8192, 14336], P('row', ('col', 'depth')), may hold values from -0.046875 to 0.046875
- gate_mask: int32 [128, 224], P('row', ('col', 'depth')), may hold values 0 or 1
- up_mask: int32 [128, 224], P('row', ('col', 'depth')), may hold values 0 or 1
- down_mask: int32 [128, 224], P('row', ('col', 'depth')), may hold values 0 or 1
Outputs:
- output: float32 [1024, 8192], P(('col', 'depth'), 'row')
- in_grad: float32 [1024, 8192], P(('col', 'depth'), 'row')
- gate_grad: float32 [8192, 14336], P('row', ('col', 'depth'))
- up_grad: float32 [8192, 14336], P('row', ('col', 'depth'))
- down_grad: float32 [8192, 14336], P('row', ('col', 'depth'))
All inputs are finite; a program needn't handle non-finite values. No bound on the sum of `gate_mask` or of `up_mask` or of `down_mask` on one device may be relied on, other than what follows from the above.
Results may differ from a plain program's by a relative error of at most 0.0029.
Values may be sent and summed in bfloat16 or wider, within the bound.
A program may use at most 384 MiB of HBM per device.

v0:
```python
import jax
import jax.numpy as jnp
from jax import lax
from jax.sharding import PartitionSpec as P


def spread(mask, block):
    mrows, mcols = mask.shape
    wide = jnp.broadcast_to(mask[:, None, :, None], (mrows, block, mcols, block))
    return wide.reshape(mrows * block, mcols * block)


def contract_last(left, right):
    return lax.dot_general(
        left, right, (((1,), (1,)), ((), ())), preferred_element_type=jnp.float32
    )


def contract_first(left, right):
    return lax.dot_general(
        left, right, (((0,), (0,)), ((), ())), preferred_element_type=jnp.float32
    )


def gather_rows(values):
    return lax.all_gather(values, "col", axis=0, tiled=True)


def reduce_rows(term_fn, count):
    return lax.psum_scatter(
        term_fn(jnp.int32(0), lax.axis_size("col") * count), "col", scatter_dimension=0, tiled=True
    )


def row_total(values):
    return lax.psum(values, "row")


def per_device(
    tokens, out_grad, gate_weight, up_weight, down_weight, gate_mask, up_mask, down_mask
):
    block = gate_weight.shape[0] // gate_mask.shape[0]
    mask_gate = spread(gate_mask, block)
    mask_up = spread(up_mask, block)
    mask_down = spread(down_mask, block)
    masked_gate = gate_weight * mask_gate.astype(jnp.bfloat16)
    masked_up = up_weight * mask_up.astype(jnp.bfloat16)
    masked_down = down_weight * mask_down.astype(jnp.bfloat16)
    w_gate, w_up, w_down = (
        lax.all_gather(masked_gate, "depth", axis=1, tiled=True),
        lax.all_gather(masked_up, "depth", axis=1, tiled=True),
        lax.all_gather(masked_down, "depth", axis=1, tiled=True),
    )
    own_rows = tokens.shape[0]
    width = w_gate.shape[1]
    inputs = gather_rows(tokens)
    gate_part = jnp.dot(inputs, w_gate, preferred_element_type=jnp.float32)
    up_part = jnp.dot(inputs, w_up, preferred_element_type=jnp.float32)
    sums = row_total(jnp.concatenate([gate_part, up_part], axis=1))
    gate = sums[:, :width]
    up = sums[:, width:]
    sig = jax.nn.sigmoid(gate)
    act = gate * sig
    hidden = (act * up).astype(jnp.bfloat16)

    def forward_term(start, count):
        return contract_last(hidden, w_down)

    output = reduce_rows(forward_term, own_rows)
    grads_in = gather_rows(out_grad)
    grad_part = jnp.dot(grads_in, w_down, preferred_element_type=jnp.float32)
    hidden_grad = row_total(grad_part)
    gate_term = (hidden_grad * up * sig * (1.0 + gate * (1.0 - sig))).astype(jnp.bfloat16)
    up_term = (hidden_grad * act).astype(jnp.bfloat16)

    def backward_term(start, count):
        return contract_last(gate_term, w_gate) + contract_last(up_term, w_up)

    in_grad = reduce_rows(backward_term, own_rows)
    grad_gate = contract_first(inputs, gate_term)
    grad_up = contract_first(inputs, up_term)
    grad_down = contract_first(grads_in, hidden)
    grad_gate, grad_up, grad_down = (
        lax.psum_scatter(grad_gate, "depth", scatter_dimension=1, tiled=True),
        lax.psum_scatter(grad_up, "depth", scatter_dimension=1, tiled=True),
        lax.psum_scatter(grad_down, "depth", scatter_dimension=1, tiled=True),
    )
    gate_grad = grad_gate * mask_gate.astype(jnp.float32)
    up_grad = grad_up * mask_up.astype(jnp.float32)
    down_grad = grad_down * mask_down.astype(jnp.float32)
    return (output, in_grad, gate_grad, up_grad, down_grad)


def solution(mesh):
    return jax.shard_map(
        per_device,
        mesh=mesh,
        in_specs=(
            P(("col", "depth"), "row"),
            P(("col", "depth"), "row"),
            P("row", ("col", "depth")),
            P("row", ("col", "depth")),
            P("row", ("col", "depth")),
            P("row", ("col", "depth")),
            P("row", ("col", "depth")),
            P("row", ("col", "depth")),
        ),
        out_specs=(
            P(("col", "depth"), "row"),
            P(("col", "depth"), "row"),
            P("row", ("col", "depth")),
            P("row", ("col", "depth")),
            P("row", ("col", "depth")),
        ),
        check_vma=False,
    )
```

profile of v0, /device:TPU:0, one launch (start us, length us, event | category | flops | bytes accessed | tf_op | source)
XLA Modules:
  0.0 962.9 jit_solution(13855527743832509890)
XLA Ops:
  7.2 0.7 all-gather.8.cloned.1.call-update
  7.9 1.4 fusion.2
  9.4 10.5 %copy.22 = bf16[2048,1792]{0,1:T(8,128)(2,1)} copy(bf16[2048,1792]{1,0:T(8,128)(2,1)} %param.11) | data formatting | bytes 14680064 | tf_op args[3]
  19.9 7.4 broadcast_in_dim.25
  27.3 20.8 %convert_element_type.54 = bf16[2048,1792]{0,1:T(8,128)(2,1)} reshape(bf16[32,64,28,64]{1,0,3,2:T(8,128)(2,1)} %broadcast_in_dim.25) | data formatting | bytes 14680064 | tf_op jit(solution)/shard_map/convert_element_type | solution.py:47
  48.1 12.8 %mul.40 = bf16[2048,1792]{0,1:T(8,128)(2,1)} multiply(bf16[2048,1792]{0,1:T(8,128)(2,1)} %copy.22, bf16[2048,1792]{0,1:T(8,128)(2,1)} %convert_element_type.54) | non-fusion elementwise | flops 3670016 | bytes 22020096 | tf_op jit(solution)/shard_map/mul | solution.py:47
  61.0 0.3 all-gather.6.cloned.1.call-start
  61.2 0.4 copy-done.6
  61.6 0.6 fusion.3
  62.3 10.6 %copy.20 = bf16[2048,1792]{0,1:T(8,128)(2,1)} copy(bf16[2048,1792]{1,0:T(8,128)(2,1)} %param.10) | data formatting | bytes 14680064 | tf_op args[2]
  73.0 10.6 %broadcast_in_dim.24 = bf16[32,64,28,64]{1,0,3,2:T(8,128)(2,1)} broadcast(bf16[32,28]{0,1:T(8,128)(2,1)S(1)} %copy.19), dimensions={0,2} | broadcast | bytes 7341824 | tf_op jit(solution)/shard_map/broadcast_in_dim | solution.py:9
  83.5 21.0 %convert_element_type.52 = bf16[2048,1792]{0,1:T(8,128)(2,1)} reshape(bf16[32,64,28,64]{1,0,3,2:T(8,128)(2,1)} %broadcast_in_dim.24) | data formatting | bytes 14680064 | tf_op jit(solution)/shard_map/convert_element_type | solution.py:46
  104.5 12.6 %mul.39 = bf16[2048,1792]{0,1:T(8,128)(2,1)} multiply(bf16[2048,1792]{0,1:T(8,128)(2,1)} %copy.20, bf16[2048,1792]{0,1:T(8,128)(2,1)} %convert_element_type.52) | non-fusion elementwise | flops 3670016 | bytes 22020096 | tf_op jit(solution)/shard_map/mul | solution.py:46
  117.2 0.5 all-gather.14.cloned.1.call-update
  117.8 0.3 all-gather.12.cloned.1.call-start
  118.1 0.6 fusion.1
  118.8 10.7 %copy.24 = bf16[2048,1792]{0,1:T(8,128)(2,1)} copy(bf16[2048,1792]{1,0:T(8,128)(2,1)} %param.12) | data formatting | bytes 14680064 | tf_op args[4]
  129.5 10.6 %broadcast_in_dim.26 = bf16[32,64,28,64]{1,0,3,2:T(8,128)(2,1)} broadcast(bf16[32,28]{0,1:T(8,128)(2,1)S(1)} %copy.23), dimensions={0,2} | broadcast | bytes 7341824 | tf_op jit(solution)/shard_map/broadcast_in_dim | solution.py:9
  140.1 21.1 %convert_element_type.57 = bf16[2048,1792]{0,1:T(8,128)(2,1)} reshape(bf16[32,64,28,64]{1,0,3,2:T(8,128)(2,1)} %broadcast_in_dim.26) | data formatting | bytes 14680064 | tf_op jit(solution)/shard_map/convert_element_type | solution.py:48
  161.2 12.5 %mul.43 = bf16[2048,1792]{0,1:T(8,128)(2,1)} multiply(bf16[2048,1792]{0,1:T(8,128)(2,1)} %copy.24, bf16[2048,1792]{0,1:T(8,128)(2,1)} %convert_element_type.57) | non-fusion elementwise | flops 3670016 | bytes 22020096 | tf_op jit(solution)/shard_map/mul | solution.py:48
  173.7 0.5 all-reduce.3.cloned.1.call-start
  174.3 15.5 %convolution_bitcast_fusion.4 = f32[512,3584]{0,1:T(8,128)} fusion(bf16[2048,3584]{0,1:T(8,128)(2,1)} %all-gather.10.cloned.1.call-done, bf16[512,2048]{1,0:T(8,128)(2,1)} %all-gather.8.cloned.1.call-done), kind=kOutput, calls=%fused_computation.10 | convolution fusion | flops 7516192768 | bytes 24117248 | tf_op jit(solution)/shard_map/dot_general | solution.py:58
  189.8 10.9 %convolution_bitcast_fusion.5 = f32[512,3584]{0,1:T(8,128)S(1)} fusion(bf16[2048,3584]{0,1:T(8,128)(2,1)} %all-gather.6.cloned.1.call-done, bf16[512,2048]{1,0:T(8,128)(2,1)S(1)} %copy-done.8), kind=kOutput, calls=%fused_computation.11 | convolution fusion | flops 7516192768 | bytes 24117248 | tf_op jit(solution)/shard_map/dot_general | solution.py:57
  200.7 9.1 pad_maximum_fusion
  209.8 12.9 %all-gather.12.cloned.1.call-done = bf16[2048,3584]{0,1:T(8,128)(2,1)} async-done(((bf16[2048,1792]{0,1:T(8,128)(2,1)}), bf16[2048,3584]{0,1:T(8,128)(2,1)}) %all-gather.12.cloned.1.call-update) | async-done | bytes 14680080 | tf_op jit(solution)/shard_map/all_gather | solution.py:52
  222.7 13.6 %convolution_bitcast_fusion.3 = f32[512,3584]{0,1:T(8,128)} fusion(bf16[2048,3584]{0,1:T(8,128)(2,1)} %all-gather.12.cloned.1.call-done, bf16[512,2048]{1,0:T(8,128)(2,1)} %all-gather.14.cloned.1.call-done), kind=kOutput, calls=%fused_computation.9 | convolution fusion | flops 7516192768 | bytes 24117248 | tf_op jit(solution)/shard_map/dot_general | solution.py:71
  236.5 393.8 %all-reduce.3.cloned.1.call-done = (f32[512,7168]{0,1:T(8,128)}, f32[512,3584]{0,1:T(8,128)}) async-done(((f32[512,7168]{0,1:T(8,128)}, f32[512,3584]{0,1:T(8,128)}), (f32[512,7168]{0,1:T(8,128)}, f32[512,3584]{0,1:T(8,128)})) %all-reduce.3.cloned.1.call-update) | async-done | bytes 22020112 | tf_op jit(solution)/shard_map/psum | solution.py:36
  630.3 11.8 %multiply_convert_fusion = (bf16[512,3584]{0,1:T(8,128)(2,1)}, bf16[512,3584]{0,1:T(8,128)(2,1)}, bf16[512,3584]{0,1:T(8,128)(2,1)S(1)}) fusion(f32[512,3584]{0,1:T(8,128)} %get-tuple-element.16, f32[512,7168]{0,1:T(8,128)} %get-tuple-element.15), kind=kLoop, calls=%fused_computation.4 | loop fusion | flops 27525120 | bytes 33030144 | tf_op jit(solution)/shard_map/convert_element_type | solution.py:74
  642.2 1.8 copy-done.1
  644.0 12.8 %convolution_bitcast_fusion = f32[2048,3584]{0,1:T(8,128)} fusion(bf16[512,3584]{0,1:T(8,128)(2,1)S(1)} %get-tuple-element.19, bf16[512,2048]{1,0:T(8,128)(2,1)S(1)} %copy-done.9), kind=kOutput, calls=%fused_computation | convolution fusion | flops 7516192768 | bytes 35127296 | tf_op jit(solution)/shard_map/dot_general | solution.py:20
  656.8 21.8 %convolution_bitcast_fusion.1 = f32[2048,3584]{0,1:T(8,128)} fusion(bf16[512,3584]{0,1:T(8,128)(2,1)} %get-tuple-element.17, bf16[512,2048]{1,0:T(8,128)(2,1)S(1)} %copy-done.8), kind=kOutput, calls=%fused_computation.1 | convolution fusion | flops 7516192768 | bytes 35127296 | tf_op jit(solution)/shard_map/dot_general | solution.py:20
  679.0 20.2 %convolution_bitcast_fusion.2 = f32[2048,3584]{0,1:T(8,128)} fusion(bf16[512,3584]{0,1:T(8,128)(2,1)} %get-tuple-element.18, bf16[512,2048]{1,0:T(8,128)(2,1)S(1)} %copy-done.8), kind=kOutput, calls=%fused_computation.2 | convolution fusion | flops 7516192768 | bytes 35127296 | tf_op jit(solution)/shard_map/dot_general | solution.py:20
  699.2 12.2 %fusion.5 = f32[512,2048]{1,0:T(8,128)S(1)} fusion(bf16[512,3584]{0,1:T(8,128)(2,1)} %get-tuple-element.18, bf16[2048,3584]{0,1:T(8,128)(2,1)} %all-gather.6.cloned.1.call-done), kind=kOutput, calls=%fused_computation.17 | convolution fusion | flops 7516192768 | bytes 22544384 | tf_op jit(solution)/shard_map/dot_general | solution.py:14
  711.5 13.9 %convolution_add_fusion = f32[512,2048]{1,0:T(8,128)} fusion(f32[512,2048]{1,0:T(8,128)S(1)} %fusion.5, bf16[512,3584]{0,1:T(8,128)(2,1)S(1)} %copy-done.2, bf16[2048,3584]{0,1:T(8,128)(2,1)} %all-gather.10.cloned.1.call-done), kind=kOutput, calls=%fused_computation.12 | convolution fusion | flops 7517241344 | bytes 26738688 | tf_op jit(solution)/shard_map/dot_general | solution.py:14
  725.5 0.3 reduce-scatter.6.cloned.1.call-start
  725.8 15.9 %fusion.4 = f32[512,2048]{1,0:T(8,128)} fusion(bf16[512,3584]{0,1:T(8,128)(2,1)} %copy-done.1, bf16[2048,3584]{0,1:T(8,128)(2,1)} %all-gather.12.cloned.1.call-done), kind=kOutput, calls=%fused_computation.16 | convolution fusion | flops 7516192768 | bytes 22544384 | tf_op jit(solution)/shard_map/dot_general | solution.py:14
  742.0 18.2 %broadcast_in_dim.29 = f32[32,64,28,64]{1,0,3,2:T(8,128)} broadcast(f32[32,28]{0,1:T(8,128)S(1)} %copy.27), dimensions={0,2} | broadcast | bytes 14683648 | tf_op jit(solution)/shard_map/broadcast_in_dim | solution.py:9
  760.2 28.2 %convert_element_type.65 = f32[2048,1792]{0,1:T(8,128)} reshape(f32[32,64,28,64]{1,0,3,2:T(8,128)} %broadcast_in_dim.29) | data formatting | bytes 29360128 | tf_op jit(solution)/shard_map/convert_element_type | solution.py:90
  788.4 14.3 %broadcast_in_dim.28 = f32[32,64,28,64]{1,0,3,2:T(8,128)} broadcast(f32[32,28]{0,1:T(8,128)S(1)} %copy.26), dimensions={0,2} | broadcast | bytes 14683648 | tf_op jit(solution)/shard_map/broadcast_in_dim | solution.py:9
  802.7 25.4 %convert_element_type.63 = f32[2048,1792]{0,1:T(8,128)} reshape(f32[32,64,28,64]{1,0,3,2:T(8,128)} %broadcast_in_dim.28) | data formatting | bytes 29360128 | tf_op jit(solution)/shard_map/convert_element_type | solution.py:89
  828.2 13.7 %broadcast_in_dim.27 = f32[32,64,28,64]{1,0,3,2:T(8,128)} broadcast(f32[32,28]{0,1:T(8,128)S(1)} %copy.25), dimensions={0,2} | broadcast | bytes 14683648 | tf_op jit(solution)/shard_map/broadcast_in_dim | solution.py:9
  841.9 25.4 %convert_element_type.61 = f32[2048,1792]{0,1:T(8,128)} reshape(f32[32,64,28,64]{1,0,3,2:T(8,128)} %broadcast_in_dim.27) | data formatting | bytes 29360128 | tf_op jit(solution)/shard_map/convert_element_type | solution.py:88
  867.3 15.3 %mul.51 = f32[2048,1792]{0,1:T(8,128)} multiply(f32[2048,1792]{0,1:T(8,128)} %reduce-scatter.14.cloned.1.call-done, f32[2048,1792]{0,1:T(8,128)} %convert_element_type.65) | non-fusion elementwise | flops 3670016 | bytes 44040192 | tf_op jit(solution)/shard_map/mul | solution.py:90
  882.6 14.3 %copy.30 = f32[2048,1792]{1,0:T(8,128)} copy(f32[2048,1792]{0,1:T(8,128)} %mul.51) | data formatting | bytes 29360128
  896.8 15.1 %mul.50 = f32[2048,1792]{0,1:T(8,128)} multiply(f32[2048,1792]{0,1:T(8,128)} %reduce-scatter.12.cloned.1.call-done, f32[2048,1792]{0,1:T(8,128)} %convert_element_type.63) | non-fusion elementwise | flops 3670016 | bytes 44040192 | tf_op jit(solution)/shard_map/mul | solution.py:89
  912.0 14.3 %copy.29 = f32[2048,1792]{1,0:T(8,128)} copy(f32[2048,1792]{0,1:T(8,128)} %mul.50) | data formatting | bytes 29360128
  926.3 15.4 %mul.49 = f32[2048,1792]{0,1:T(8,128)} multiply(f32[2048,1792]{0,1:T(8,128)} %reduce-scatter.10.cloned.1.call-done, f32[2048,1792]{0,1:T(8,128)} %convert_element_type.61) | non-fusion elementwise | flops 3670016 | bytes 44040192 | tf_op jit(solution)/shard_map/mul | solution.py:88
  941.7 14.3 %copy.28 = f32[2048,1792]{1,0:T(8,128)} copy(f32[2048,1792]{0,1:T(8,128)} %mul.49) | data formatting | bytes 29360128
  (49 shorter events, 1.4 us)
Async XLA Ops:
  7.2 167.1 %all-gather.8.cloned.1.call-start = ((), (), s32[]{:S(2)}) async-start(), calls=%async_computation.6 | async-start | bytes 2621440 | tf_op jit(solution)/shard_map/all_gather | solution.py:26
  7.9 166.4 %all-gather.10.cloned.1.call-start = ((), (), s32[]{:S(2)}) async-start(), calls=%async_computation.7 | async-start | bytes 22020096 | tf_op jit(solution)/shard_map/all_gather | solution.py:51
  60.9 0.7 copy-start.6
  61.0 128.9 %all-gather.6.cloned.1.call-start = ((), (), s32[]{:S(2)}) async-start(), calls=%async_computation.5 | async-start | bytes 22020096 | tf_op jit(solution)/shard_map/all_gather | solution.py:50
  117.2 0.9 copy-start.7
  117.2 92.6 %all-gather.14.cloned.1.call-start = ((), (), s32[]{:S(2)}) async-start(), calls=%async_computation.10 | async-start | bytes 2621440 | tf_op jit(solution)/shard_map/all_gather | solution.py:26
  117.8 104.9 %all-gather.12.cloned.1.call-start = ((), (), s32[]{:S(2)}) async-start(), calls=%async_computation.8 | async-start | bytes 22020096 | tf_op jit(solution)/shard_map/all_gather | solution.py:52
  173.7 456.6 %all-reduce.3.cloned.1.call-start = ((), (), s32[]{:S(2)}) async-start(), calls=%async_computation.15 | async-start | bytes 44040192 | tf_op jit(solution)/shard_map/psum | solution.py:36
  174.3 15.6 %copy-start.8 = (bf16[512,2048]{1,0:T(8,128)(2,1)S(1)}, bf16[512,2048]{1,0:T(8,128)(2,1)}, u32[]{:S(2)}) copy-start(bf16[512,2048]{1,0:T(8,128)(2,1)} %all-gather.8.cloned.1.call-done) | copy-start | bytes 6291460
  189.8 10.9 %copy-start = (f32[512,3584]{0,1:T(8,128)S(1)}, f32[512,3584]{0,1:T(8,128)}, u32[]{:S(2)}) copy-start(f32[512,3584]{0,1:T(8,128)} %convolution_bitcast_fusion.4) | copy-start | bytes 22020100
  236.3 631.0 %reduce-scatter.14.cloned.1.call-start = ((), (), s32[]{:S(2)}) async-start(), calls=%async_computation.14 | async-start | bytes 44040192 | tf_op jit(solution)/shard_map/reduce_scatter | solution.py:86
  630.3 13.7 %copy-start.9 = (bf16[512,2048]{1,0:T(8,128)(2,1)S(1)}, bf16[512,2048]{1,0:T(8,128)(2,1)}, u32[]{:S(2)}) copy-start(bf16[512,2048]{1,0:T(8,128)(2,1)} %all-gather.14.cloned.1.call-done) | copy-start | bytes 6291460
  642.2 1.8 copy-start.1
  656.8 240.0 %reduce-scatter.12.cloned.1.call-start = ((), (), s32[]{:S(2)}) async-start(), calls=%async_computation.13 | async-start | bytes 44040192 | tf_op jit(solution)/shard_map/reduce_scatter | solution.py:85
  678.7 247.6 %reduce-scatter.10.cloned.1.call-start = ((), (), s32[]{:S(2)}) async-start(), calls=%async_computation.12 | async-start | bytes 44040192 | tf_op jit(solution)/shard_map/reduce_scatter | solution.py:84
  699.2 256.8 %reduce-scatter.8.cloned.1.call-start = ((), (), s32[]{:S(2)}) async-start(), calls=%async_computation.11 | async-start | bytes 5242880 | tf_op jit(solution)/shard_map/reduce_scatter | solution.py:30
  699.2 12.3 %copy-start.2 = (bf16[512,3584]{0,1:T(8,128)(2,1)S(1)}, bf16[512,3584]{0,1:T(8,128)(2,1)}, u32[]{:S(2)}) copy-start(bf16[512,3584]{0,1:T(8,128)(2,1)} %get-tuple-element.17) | copy-start | bytes 11010052
  725.4 16.3 %copy-start.4 = (f32[32,28]{1,0:T(8,128)S(1)}, f32[32,28]{1,0:T(8,128)}, u32[]{:S(2)}) copy-start(f32[32,28]{1,0:T(8,128)} %get-tuple-element.24) | copy-start | bytes 10756
  725.4 16.3 %copy-start.3 = (f32[32,28]{1,0:T(8,128)S(1)}, f32[32,28]{1,0:T(8,128)}, u32[]{:S(2)}) copy-start(f32[32,28]{1,0:T(8,128)} %get-tuple-element.22) | copy-start | bytes 10756
  725.5 16.4 %copy-start.5 = (f32[32,28]{1,0:T(8,128)S(1)}, f32[32,28]{1,0:T(8,128)}, u32[]{:S(2)}) copy-start(f32[32,28]{1,0:T(8,128)} %get-tuple-element.20) | copy-start | bytes 10756
  725.5 230.5 %reduce-scatter.6.cloned.1.call-start = ((), (), s32[]{:S(2)}) async-start(), calls=%async_computation.9 | async-start | bytes 5242880 | tf_op jit(solution)/shard_map/reduce_scatter | solution.py:30
Sparse Core Ops, SparseCore 0:
  9.6 48.6 all-gather.7
  61.1 29.7 all-gather.9
  117.3 29.5 all-gather.5
  148.4 47.0 all-gather.13
  196.9 25.7 all-gather.11
  236.4 393.8 all-reduce.2
  656.9 40.2 reduce-scatter.13
  699.7 41.3 reduce-scatter.11
  743.5 41.3 reduce-scatter.9
  787.7 78.0 reduce-scatter.7
  868.6 77.2 reduce-scatter.5
where the time goes:
time: 974 us; the launch traced here: 963 us
  waiting for transfers between devices  408 us (42%)
  local copies, waits for them, and re-layouts  294 us (30%)
  matrix products  137 us (14%)
  other arithmetic  107 us (11%)
  between operations  14.4 us (1%)
    psum x1, waiting for transfers between devices, row_total(): return lax.psum(values, 'row')  394 us
    unnamed x26, local copies, waits for them, and re-layouts  76.9 us
    broadcast_in_dim x6, local copies, waits for them, and re-layouts, spread(): jnp.broadcast_to(mask[:, None, :, None], (mrows, block, mcols, block))  74.9 us
    dot_general x3, matrix products, contract_first(): lax.dot_general(left, right, (((0,), (0,)), ((), ())), preferred_element_...  54.8 us
    dot_general x3, matrix products, contract_last(): lax.dot_general(left, right, (((1,), (1,)), ((), ())), preferred_element_...  42.1 us
    convert_element_type x2, local copies, waits for them, and re-layouts, per_device(): down_grad = grad_down * mask_down.astype(jnp.float32)  28.3 us
    convert_element_type x2, local copies, waits for them, and re-layouts, per_device(): up_grad = grad_up * mask_up.astype(jnp.float32)  25.5 us
    convert_element_type x2, local copies, waits for them, and re-layouts, per_device(): gate_grad = grad_gate * mask_gate.astype(jnp.float32)  25.5 us
  transfers between devices with their start and end apart: 11, of which 2 were waited for; matrix products, arithmetic and copies ran while one was open for 52% of the time, Pallas kernels for 0%

commit v1 on v0

v1 whole, which is shorter than its diff:
```python
import jax
import jax.numpy as jnp
from jax import lax
from jax.sharding import PartitionSpec as P

SPLIT = 2
F32 = jnp.float32
BF16 = jnp.bfloat16
F16 = jnp.float16
F16_ROOM = 2.0**14


def contract_last(left, right):
    return lax.dot_general(left, right, (((1,), (1,)), ((), ())), preferred_element_type=F32)


def contract_first(left, right):
    return lax.dot_general(left, right, (((0,), (0,)), ((), ())), preferred_element_type=F32)


def wide_columns(mask, block):
    cols = mask.shape[1]
    unit = jnp.arange(cols)[:, None] == (jnp.arange(cols * block) // block)[None, :]
    return jnp.dot(mask.astype(BF16), unit.astype(BF16), preferred_element_type=F32)


def apply_mask(values, wide):
    rows, cols = values.shape
    shaped = values.reshape(wide.shape[0], rows // wide.shape[0], cols)
    return (shaped * wide.astype(values.dtype)[:, None, :]).reshape(rows, cols)


def full_mask(wide, rows):
    count, cols = wide.shape
    spread = jnp.broadcast_to(wide.astype(BF16)[:, None, :], (count, rows // count, cols))
    return lax.optimization_barrier(spread.reshape(rows, cols))


def half_at(values, which):
    count = values.shape[0] // 2
    return lax.dynamic_slice_in_dim(values, which * count, count, 0)


def join_halves(mine, other, which):
    first = jnp.where(which == 0, mine, other)
    second = jnp.where(which == 0, other, mine)
    return jnp.concatenate([first, second], axis=0)


class RowGroup:
    def __init__(self):
        self.size = lax.axis_size("row")
        self.cores = lax.axis_size("depth")
        self.bits = self.size.bit_length() - 1
        assert 1 << self.bits == self.size
        me, core = lax.axis_index("row"), lax.axis_index("depth")
        self.mine = []
        for stage in range(self.bits):
            bit = (stage + core * (self.bits // 2)) % self.bits
            self.mine.append((me >> bit) & 1)

    def swap(self, values, stage):
        pairs = []
        for r in range(self.size):
            for d in range(self.cores):
                bit = (stage + d * (self.bits // 2)) % self.bits
                pairs.append((r * self.cores + d, (r ^ (1 << bit)) * self.cores + d))
        return lax.ppermute(values, ("row", "depth"), pairs)

    def scatter_product(self, left, right, bound):
        scale, back = F16_ROOM / bound, bound / F16_ROOM
        bit = self.mine[0]
        away = jnp.dot(half_at(left, 1 - bit), right, preferred_element_type=F32)
        landed = self.swap((away * scale).astype(F16), 0)
        total = jnp.dot(half_at(left, bit), right, preferred_element_type=F32)
        total = total + landed.astype(F32) * back
        for stage in range(1, self.bits):
            bit = self.mine[stage]
            landed = self.swap((half_at(total, 1 - bit) * scale).astype(F16), stage)
            total = half_at(total, bit) + landed.astype(F32) * back
        return total

    def gather(self, values):
        for stage in reversed(range(self.bits)):
            values = join_halves(values, self.swap(values, stage), self.mine[stage])
        return values


def gather_tokens(values):
    over_col = lax.all_gather(values, "col", axis=0)
    both = lax.all_gather(over_col, "depth", axis=1)
    return both.reshape(-1, values.shape[1])


def scatter_tokens(term):
    cols, cores = lax.axis_size("col"), lax.axis_size("depth")
    assert cores == 2
    core, me = lax.axis_index("depth"), lax.axis_index("col")

    def rows_of(which):
        def select(values):
            shaped = values.reshape(cols, cores, -1, values.shape[1])
            return lax.dynamic_index_in_dim(shaped, which, 1, keepdims=False).reshape(-1, values.shape[1])

        return select

    landed = lax.ppermute(term(rows_of(1 - core)), "depth", [(0, 1), (1, 0)])
    total = term(rows_of(core)) + landed
    width = total.shape[1]
    bits = cols.bit_length() - 1
    assert 1 << bits == cols
    for bit in range(bits):
        side = (me >> bit) & 1
        shaped = total.reshape(cols >> (bit + 1), 2, -1, width)

        def pick(which):
            return lax.dynamic_index_in_dim(shaped, which, 1, keepdims=False).reshape(-1, width)

        pairs = [(c, c ^ (1 << bit)) for c in range(cols)]
        landed = lax.ppermute(pick(1 - side).astype(BF16), "col", pairs)
        total = pick(side) + landed.astype(F32)
    return total


def product_bounds(tokens, out_grad, gate_weight, up_weight, down_weight):
    tops = [jnp.max(jnp.abs(v)).astype(F32) for v in (tokens, out_grad, gate_weight, up_weight, down_weight)]
    tops = lax.pmax(jnp.stack(tops), ("row", "col", "depth"))
    features = tokens.shape[1] * lax.axis_size("row")
    return [
        jnp.maximum(tops[a] * tops[b] * features, 1e-30) for a, b in ((0, 2), (0, 3), (1, 4))
    ]


def per_device(
    tokens, out_grad, gate_weight, up_weight, down_weight, gate_mask, up_mask, down_mask
):
    block = gate_weight.shape[0] // gate_mask.shape[0]
    row = RowGroup()
    own = tokens.shape[0] // SPLIT
    inputs, grads_in = [], []
    for part in range(SPLIT):
        inputs.append(gather_tokens(tokens[part * own : (part + 1) * own]))
        grads_in.append(gather_tokens(out_grad[part * own : (part + 1) * own]))
    gate_bound, up_bound, hidden_bound = product_bounds(
        tokens, out_grad, gate_weight, up_weight, down_weight
    )
    wide_gate = wide_columns(gate_mask, block)
    wide_up = wide_columns(up_mask, block)
    wide_down = wide_columns(down_mask, block)
    w_gate = apply_mask(gate_weight, wide_gate)
    w_up = apply_mask(up_weight, wide_up)
    w_down = apply_mask(down_weight, wide_down)

    rows = gate_weight.shape[0]
    full_gate, full_up, full_down = (
        full_mask(wide_gate, rows),
        full_mask(wide_up, rows),
        full_mask(wide_down, rows),
    )

    hiddens, gate_terms, up_terms, outputs, in_grads = [], [], [], [], []
    for part in range(SPLIT):
        gate = row.scatter_product(inputs[part], w_gate, gate_bound)
        up = row.scatter_product(inputs[part], w_up, up_bound)
        sig = jax.nn.sigmoid(gate)
        act = gate * sig
        hidden = row.gather((act * up).astype(BF16))
        hidden_grad = row.scatter_product(grads_in[part], w_down, hidden_bound)
        gate_term = row.gather((hidden_grad * up * sig * (1.0 + gate * (1.0 - sig))).astype(BF16))
        up_term = row.gather((hidden_grad * act).astype(BF16))
        outputs.append(scatter_tokens(lambda select: contract_last(select(hidden), w_down)))
        in_grads.append(
            scatter_tokens(
                lambda select: contract_last(select(gate_term), w_gate)
                + contract_last(select(up_term), w_up)
            )
        )
        hiddens.append(hidden)
        gate_terms.append(gate_term)
        up_terms.append(up_term)

    def joined(parts):
        return jnp.concatenate(parts, axis=0)

    all_inputs, all_grads = joined(inputs), joined(grads_in)
    gate_grad = contract_first(all_inputs, joined(gate_terms)) * full_gate.astype(F32)
    up_grad = contract_first(all_inputs, joined(up_terms)) * full_up.astype(F32)
    down_grad = contract_first(all_grads, joined(hiddens)) * full_down.astype(F32)
    return (joined(outputs), joined(in_grads), gate_grad, up_grad, down_grad)


def solution(mesh):
    tokens, weights = P(("col", "depth"), "row"), P("row", ("col", "depth"))
    return jax.shard_map(
        per_device,
        mesh=mesh,
        in_specs=(tokens,) * 2 + (weights,) * 6,
        out_specs=(tokens,) * 2 + (weights,) * 3,
        check_vma=False,
    )
```

time: 974 us -> 561 us (0.58)
  local copies, waits for them, and re-layouts: 294 us -> 25.5 us
  waiting for transfers between devices: 408 us -> 229 us
  other arithmetic: 107 us -> 42.2 us
  starting transfers between devices: 2.01 us -> 53.4 us
  blocking collectives: 0 us -> 40.3 us
    psum x1 -> x0, waiting for transfers between devices: 394 us -> none  [row_total(): return lax.psum(values, 'row')]
    convert_element_type x12 -> x8, local copies, waits for them, and re-layouts: 143 us -> 0.43 us  [scatter_tokens(): landed = lax.ppermute(pick(1 - side).astype(BF16), 'col', pairs)]
    ppermute x0 -> x36, waiting for transfers between devices: none -> 140 us  [the longest x24 82.6 us: swap(): return lax.ppermute(values, ('row', 'depth'), pairs)]
    unnamed x26 -> x82, local copies, waits for them, and re-layouts: 76.9 us -> 1.51 us
    broadcast_in_dim x6 -> x0, local copies, waits for them, and re-layouts: 74.9 us -> none  [spread(): jnp.broadcast_to(mask[:, None, :, None], (mrows, block, mcols, block))]
    all_gather x5 -> x8, waiting for transfers between devices: 12.9 us -> 87.5 us  [the longest x4 87.5 us: gather_tokens(): over_col = lax.all_gather(values, 'col', axis=0)]
    mul x6 -> x2, other arithmetic: 83.8 us -> 14.9 us  [apply_mask(): return (shaped * wide.astype(values.dtype)[:, None, :]).reshape(rows, cols)]
    ppermute x0 -> x36, starting transfers between devices: none -> 53 us  [the longest x24 34.4 us: swap(): return lax.ppermute(values, ('row', 'depth'), pairs)]
  transfers between devices with their start and end apart: 11 -> 44, of which waited for: 2 -> 19; matrix products, arithmetic and copies ran while one was open for 52% -> 37% of each run, Pallas kernels for 0% -> 0%
where the time goes in v1:
time: 561 us; the launch traced here: 554 us
  waiting for transfers between devices  229 us (41%)
  matrix products  144 us (26%)
  starting transfers between devices  53.4 us (10%)
  other arithmetic  42.2 us (8%)
  blocking collectives  40.3 us (7%)
  local copies, waits for them, and re-layouts  25.5 us (5%)
  between operations  19.2 us (3%)
    all_gather x4, waiting for transfers between devices, gather_tokens(): over_col = lax.all_gather(values, 'col', axis=0)  87.5 us
    ppermute x24, waiting for transfers between devices, swap(): return lax.ppermute(values, ('row', 'depth'), pairs)  82.6 us
    ppermute x8, waiting for transfers between devices, scatter_tokens(): landed = lax.ppermute(pick(1 - side).astype(BF16), 'col', pairs)  57.9 us
    dot_general x3, matrix products, contract_first(): lax.dot_general(left, right, (((0,), (0,)), ((), ())), preferred_element_...  47.8 us
    dot_general x12, matrix products, contract_last(): lax.dot_general(left, right, (((1,), (1,)), ((), ())), preferred_element_...  44.9 us
    pmax x1, blocking collectives, product_bounds(): tops = lax.pmax(jnp.stack(tops), ('row', 'col', 'depth'))  40.3 us
    ppermute x24, starting transfers between devices, swap(): return lax.ppermute(values, ('row', 'depth'), pairs)  34.4 us
    dot_general x6, matrix products, scatter_product(): away = jnp.dot(half_at(left, 1 - bit), right, preferred_element_type=F32)  31.2 us
  transfers between devices with their start and end apart: 44, of which 19 were waited for; matrix products, arithmetic and copies ran while one was open for 37% of the time, Pallas kernels for 0%

profile of v1, /device:TPU:0, one launch (start us, length us, event | category | flops | bytes accessed | tf_op | source)
XLA Modules:
  0.0 553.8 jit_solution(5608433072805093760)
XLA Ops:
  12.4 28.4 %all-gather.29.cloned.1.call-done = bf16[256,2048]{1,0:T(8,128)(2,1)} async-done(((bf16[64,2048]{1,0:T(8,128)(2,1)}), bf16[256,2048]{1,0:T(8,128)(2,1)}) %all-gather.29.cloned.1.call-update) | async-done | bytes 1048592 | tf_op jit(solution)/shard_map/all_gather | solution.py:90
  40.9 29.5 %all-gather.21.cloned.1.call-done = bf16[256,2048]{1,0:T(8,128)(2,1)} async-done(((bf16[64,2048]{1,0:T(8,128)(2,1)}), bf16[256,2048]{1,0:T(8,128)(2,1)}) %all-gather.21.cloned.1.call-update) | async-done | bytes 1048592 | tf_op jit(solution)/shard_map/all_gather | solution.py:90
  70.5 29.5 %all-gather.17.cloned.1.call-done = bf16[256,2048]{1,0:T(8,128)(2,1)} async-done(((bf16[64,2048]{1,0:T(8,128)(2,1)}), bf16[256,2048]{1,0:T(8,128)(2,1)}) %all-gather.17.cloned.1.call-update) | async-done | bytes 1048592 | tf_op jit(solution)/shard_map/all_gather | solution.py:90
  100.3 9.1 %bitcast_multiply_fusion = (bf16[2048,1792]{1,0:T(8,128)(2,1)}, bf16[]{:T(256)}) fusion(bf16[2048,1792]{1,0:T(8,128)(2,1)} %param.12, bf16[32,1792]{1,0:T(8,128)(2,1)S(1)} %fusion.34), kind=kLoop, calls=%fused_computation.31 | loop fusion | flops 11010047 | bytes 14794754 | tf_op jit(solution)/shard_map/mul | solution.py:30
  109.6 5.8 %bitcast_multiply_fusion.2 = (bf16[2048,1792]{1,0:T(8,128)(2,1)}, bf16[]{:T(256)}) fusion(bf16[2048,1792]{1,0:T(8,128)(2,1)S(1)} %bitcast.122, bf16[32,1792]{1,0:T(8,128)(2,1)S(1)} %fusion.32), kind=kLoop, calls=%fused_computation.33 | loop fusion | flops 11010047 | bytes 14794754 | tf_op jit(solution)/shard_map/mul | solution.py:30
  115.6 9.1 %abs_reduce_fusion.1 = (bf16[]{:T(256)}, bf16[2048,1792]{1,0:T(8,128)(2,1)}) fusion(bf16[2048,1792]{1,0:T(8,128)(2,1)} %param.11, bf16[32,1792]{1,0:T(8,128)(2,1)S(1)} %fusion.33), kind=kLoop, calls=%fused_computation.4 | loop fusion | flops 11010047 | bytes 14794754 | tf_op jit(solution)/shard_map/reduce_max | solution.py:126
  126.1 3.4 stack.31
  129.5 40.3 %pmax.7 = f32[5]{0:T(128)S(1)} all-reduce(bf16[5]{0:T(256)(128)(2,1)S(1)} %stack.31), channel_id=1, replica_groups=mesh['row'=4,'col'=4,'depth'=2] {'row','col','depth'}, use_global_device_ids=true, to_apply=%region_5.6 | all-reduce | flops 5 | bytes 30 | tf_op jit(solution)/shard_map/pmax | solution.py:127
  174.2 3.5 mul.261
  177.8 3.5 mul.278
  181.3 3.5 mul.292
  184.8 6.4 %fusion.31 = f16[256,1792]{1,0:T(8,128)(2,1)} fusion(bf16[2048,1792]{1,0:T(8,128)(2,1)} %get-tuple-element.5, bf16[512,2048]{1,0:T(8,128)(2,1)} %bitcast.178, s32[]{:T(128)S(6)} %select_n.211, f32[]{:T(128)} %bitcast.39), kind=kOutput, calls=%fused_computation.53 | convolution fusion | flops 1879965696 | bytes 9306628 | tf_op jit(solution)/shard_map/dot_general | solution.py:73
  193.5 6.5 %fusion.28 = f16[256,1792]{1,0:T(8,128)(2,1)} fusion(bf16[2048,1792]{1,0:T(8,128)(2,1)} %get-tuple-element.7, bf16[512,2048]{1,0:T(8,128)(2,1)} %bitcast.181, s32[]{:T(128)S(6)} %select_n.211, f32[]{:T(128)} %bitcast.9), kind=kOutput, calls=%fused_computation.50 | convolution fusion | flops 1879965696 | bytes 9306628 | tf_op jit(solution)/shard_map/dot_general | solution.py:73
  200.0 6.5 %fusion.26 = f16[256,1792]{1,0:T(8,128)(2,1)} fusion(bf16[2048,1792]{1,0:T(8,128)(2,1)} %get-tuple-element.7, bf16[512,2048]{1,0:T(8,128)(2,1)} %bitcast.187, s32[]{:T(128)S(6)} %select_n.211, f32[]{:T(128)} %bitcast.9), kind=kOutput, calls=%fused_computation.48 | convolution fusion | flops 1879965696 | bytes 9306628 | tf_op jit(solution)/shard_map/dot_general | solution.py:73
  214.7 5.6 %fusion.30 = f16[256,1792]{1,0:T(8,128)(2,1)S(1)} fusion(bf16[2048,1792]{1,0:T(8,128)(2,1)} %get-tuple-element.5, bf16[512,2048]{1,0:T(8,128)(2,1)} %bitcast.193, s32[]{:T(128)S(6)} %select_n.211, f32[]{:T(128)} %bitcast.39), kind=kOutput, calls=%fused_computation.52 | convolution fusion | flops 1879965696 | bytes 9306628 | tf_op jit(solution)/shard_map/dot_general | solution.py:73
  223.1 5.5 multiply_add_fusion
  232.9 10.3 %collective-permute-done.11 = f16[256,1792]{1,0:T(8,128)(2,1)S(1)} collective-permute-done((f16[256,1792]{1,0:T(8,128)(2,1)}, f16[256,1792]{1,0:T(8,128)(2,1)S(1)}, u32[]{:S(2)}, u32[]{:S(2)}) %collective-permute-start.11) | collective-permute-done | bytes 917536 | tf_op jit(solution)/shard_map/ppermute | solution.py:68
  244.1 3.4 multiply_add_fusion.2
  247.6 10.0 %collective-permute-done.18 = f16[256,1792]{1,0:T(8,128)(2,1)S(1)} collective-permute-done((f16[256,1792]{1,0:T(8,128)(2,1)S(1)}, f16[256,1792]{1,0:T(8,128)(2,1)S(1)}, u32[]{:S(2)}, u32[]{:S(2)}) %collective-permute-start.18) | collective-permute-done | bytes 917536 | tf_op jit(solution)/shard_map/ppermute | solution.py:68
  261.5 11.0 %collective-permute-done = f16[256,1792]{1,0:T(8,128)(2,1)S(1)} collective-permute-done((f16[256,1792]{1,0:T(8,128)(2,1)S(1)}, f16[256,1792]{1,0:T(8,128)(2,1)S(1)}, u32[]{:S(2)}, u32[]{:S(2)}) %collective-permute-start) | collective-permute-done | bytes 917536 | tf_op jit(solution)/shard_map/ppermute | solution.py:68
  274.8 3.3 multiply_add_fusion.5
  278.2 11.0 %collective-permute-done.2 = f16[256,1792]{1,0:T(8,128)(2,1)} collective-permute-done((f16[256,1792]{1,0:T(8,128)(2,1)S(1)}, f16[256,1792]{1,0:T(8,128)(2,1)}, u32[]{:S(2)}, u32[]{:S(2)}) %collective-permute-start.2) | collective-permute-done | bytes 917536 | tf_op jit(solution)/shard_map/ppermute | solution.py:68
  290.4 3.2 multiply_add_fusion.4
  297.7 4.9 collective-permute-done.3
  309.2 8.0 %collective-permute-done.4 = bf16[128,1792]{1,0:T(8,128)(2,1)S(1)} collective-permute-done((bf16[128,1792]{1,0:T(8,128)(2,1)S(1)}, bf16[128,1792]{1,0:T(8,128)(2,1)S(1)}, u32[]{:S(2)}, u32[]{:S(2)}) %collective-permute-start.4) | collective-permute-done | bytes 458784 | tf_op jit(solution)/shard_map/ppermute | solution.py:68
  319.9 7.1 %collective-permute-done.31 = bf16[128,1792]{1,0:T(8,128)(2,1)S(1)} collective-permute-done((bf16[128,1792]{1,0:T(8,128)(2,1)S(1)}, bf16[128,1792]{1,0:T(8,128)(2,1)S(1)}, u32[]{:S(2)}, u32[]{:S(2)}) %collective-permute-start.31) | collective-permute-done | bytes 458784 | tf_op jit(solution)/shard_map/ppermute | solution.py:68
  329.8 7.1 %collective-permute-done.29 = bf16[128,1792]{1,0:T(8,128)(2,1)S(1)} collective-permute-done((bf16[128,1792]{1,0:T(8,128)(2,1)S(1)}, bf16[128,1792]{1,0:T(8,128)(2,1)S(1)}, u32[]{:S(2)}, u32[]{:S(2)}) %collective-permute-start.29) | collective-permute-done | bytes 458784 | tf_op jit(solution)/shard_map/ppermute | solution.py:68
  340.5 6.1 %collective-permute-done.22 = bf16[128,1792]{1,0:T(8,128)(2,1)S(1)} collective-permute-done((bf16[128,1792]{1,0:T(8,128)(2,1)S(1)}, bf16[128,1792]{1,0:T(8,128)(2,1)S(1)}, u32[]{:S(2)}, u32[]{:S(2)}) %collective-permute-start.22) | collective-permute-done | bytes 458784 | tf_op jit(solution)/shard_map/ppermute | solution.py:68
  350.3 6.1 %collective-permute-done.20 = bf16[128,1792]{1,0:T(8,128)(2,1)S(1)} collective-permute-done((bf16[128,1792]{1,0:T(8,128)(2,1)S(1)}, bf16[128,1792]{1,0:T(8,128)(2,1)S(1)}, u32[]{:S(2)}, u32[]{:S(2)}) %collective-permute-start.20) | collective-permute-done | bytes 458784 | tf_op jit(solution)/shard_map/ppermute | solution.py:68
  362.7 4.6 fusion.99
  367.4 3.4 fusion.98
  378.6 3.5 convolution_add_fusion
  389.9 3.4 convolution_add_fusion.2
  393.3 6.7 %collective-permute-start.24 = (f32[256,2048]{1,0:T(8,128)}, f32[256,2048]{1,0:T(8,128)}, u32[]{:S(2)}, u32[]{:S(2)}) collective-permute-start(f32[256,2048]{1,0:T(8,128)} %convolution_add_fusion.2), channel_id=1, source_target_pairs={{0,1},{1,0},{2,3},{3,2},{4,5},{5,4},{6,7},{7,6},{8,9},{9,8},{10,11... | collective-permute-start | bytes 6291464 | tf_op jit(solution)/shard_map/ppermute | solution.py:107
  400.0 16.1 %convert_multiply_fusion.2 = f32[2048,1792]{1,0:T(8,128)} fusion(bf16[2048,1792]{1,0:T(8,128)(2,1)} %bitcast.135, bf16[256,1792]{1,0:T(8,128)(2,1)} %copy-done.3, bf16[256,1792]{1,0:T(8,128)(2,1)} %copy-done.2, bf16[256,1792]{1,0:T(8,128)(2,1)} %copy-done.7, bf16[256,1792]{1,0:T(8,128)(2,1)} %copy-done.6, bf16[512,2048]{1,0:T(8,128)(2,1)} %bitcast.182, ...), kind=kOutput, calls=%fused_computation.2 | convolution fusion | flops 7546601472 | bytes 29884416 | tf_op jit(solution)/shard_map/dot_general | solution.py:18
  416.1 15.9 %convert_multiply_fusion.1 = f32[2048,1792]{1,0:T(8,128)} fusion(bf16[2048,1792]{1,0:T(8,128)(2,1)} %bitcast.134, bf16[256,1792]{1,0:T(8,128)(2,1)S(1)} %copy-done.1, bf16[256,1792]{1,0:T(8,128)(2,1)S(1)} %get-tuple-element.29, bf16[256,1792]{1,0:T(8,128)(2,1)} %copy-done.5, bf16[256,1792]{1,0:T(8,128)(2,1)} %copy-done.4, bf16[512,2048]{1,0:T(8,128)(2,1)} %bitcast.183, ...), kind=kOutput, calls=%fused_computation.1 | convolution fusion | flops 7546601472 | bytes 29884416 | tf_op jit(solution)/shard_map/dot_general | solution.py:18
  432.0 15.8 %convert_multiply_fusion = f32[2048,1792]{1,0:T(8,128)} fusion(bf16[2048,1792]{1,0:T(8,128)(2,1)} %bitcast.133, bf16[512,2048]{1,0:T(8,128)(2,1)} %bitcast.179, bf16[512,2048]{1,0:T(8,128)(2,1)} %bitcast.194, bf16[256,1792]{1,0:T(8,128)(2,1)S(1)} %get-tuple-element.40, bf16[256,1792]{1,0:T(8,128)(2,1)S(1)} %get-tuple-element.39, ...), kind=kOutput, calls=%fused_computation | convolution fusion | flops 7546601472 | bytes 29884416 | tf_op jit(solution)/shard_map/dot_general | solution.py:18
  447.9 5.3 fusion.102
  453.2 5.3 fusion.100
  458.6 3.8 convolution_add_fusion.4
  463.6 3.8 convolution_add_fusion.5
  468.5 3.7 fusion.25
  473.7 3.7 fusion.24
  481.6 12.5 %collective-permute-done.7 = bf16[128,2048]{1,0:T(8,128)(2,1)S(1)} collective-permute-done((bf16[128,2048]{1,0:T(8,128)(2,1)S(1)}, bf16[128,2048]{1,0:T(8,128)(2,1)S(1)}, u32[]{:S(2)}, u32[]{:S(2)}) %collective-permute-start.7) | collective-permute-done | bytes 524320 | tf_op jit(solution)/shard_map/ppermute | solution.py:120
  495.8 15.2 %collective-permute-done.34 = bf16[128,2048]{1,0:T(8,128)(2,1)S(1)} collective-permute-done((bf16[128,2048]{1,0:T(8,128)(2,1)S(1)}, bf16[128,2048]{1,0:T(8,128)(2,1)S(1)}, u32[]{:S(2)}, u32[]{:S(2)}) %collective-permute-start.34) | collective-permute-done | bytes 524320 | tf_op jit(solution)/shard_map/ppermute | solution.py:120
  512.7 8.8 %collective-permute-done.25 = bf16[128,2048]{1,0:T(8,128)(2,1)S(1)} collective-permute-done((bf16[128,2048]{1,0:T(8,128)(2,1)S(1)}, bf16[128,2048]{1,0:T(8,128)(2,1)S(1)}, u32[]{:S(2)}, u32[]{:S(2)}) %collective-permute-start.25) | collective-permute-done | bytes 524320 | tf_op jit(solution)/shard_map/ppermute | solution.py:120
  523.2 16.8 %collective-permute-done.35 = bf16[64,2048]{1,0:T(8,128)(2,1)S(1)} collective-permute-done((bf16[64,2048]{1,0:T(8,128)(2,1)S(1)}, bf16[64,2048]{1,0:T(8,128)(2,1)S(1)}, u32[]{:S(2)}, u32[]{:S(2)}) %collective-permute-start.35) | collective-permute-done | bytes 262176 | tf_op jit(solution)/shard_map/ppermute | solution.py:120
  541.2 4.4 collective-permute-done.26
  (237 shorter events, 94.0 us)
Async XLA Ops:
  7.2 33.6 %all-gather.29.cloned.1.call-start = ((), (), s32[]{:S(2)}) async-start(), calls=%async_computation.6 | async-start | bytes 1310720 | tf_op jit(solution)/shard_map/all_gather | solution.py:90
  9.1 61.3 %all-gather.21.cloned.1.call-start = ((), (), s32[]{:S(2)}) async-start(), calls=%async_computation.2 | async-start | bytes 1310720 | tf_op jit(solution)/shard_map/all_gather | solution.py:90
  11.0 89.1 %copy-start.16 = (s32[32,28]{1,0:T(8,128)S(1)}, s32[32,28]{1,0:T(8,128)}, u32[]{:S(2)}) copy-start(s32[32,28]{1,0:T(8,128)} %param.15) | copy-start | bytes 10756
  11.0 89.0 %all-gather.17.cloned.1.call-start = ((), (), s32[]{:S(2)}) async-start(), calls=%async_computation | async-start | bytes 1310720 | tf_op jit(solution)/shard_map/all_gather | solution.py:90
  11.8 172.9 %all-gather.25.cloned.1.call-start = ((), (), s32[]{:S(2)}) async-start(), calls=%async_computation.4 | async-start | bytes 1310720 | tf_op jit(solution)/shard_map/all_gather | solution.py:90
  12.4 172.4 %all-gather.31.cloned.1.call-start = ((), (), s32[]{:S(2)}) async-start(), calls=%async_computation.7 | async-start | bytes 3145728 | tf_op jit(solution)/shard_map/all_gather | solution.py:91
  40.8 152.6 %all-gather.23.cloned.1.call-start = ((), (), s32[]{:S(2)}) async-start(), calls=%async_computation.3 | async-start | bytes 3145728 | tf_op jit(solution)/shard_map/all_gather | solution.py:91
  70.4 129.6 %all-gather.19.cloned.1.call-start = ((), (), s32[]{:S(2)}) async-start(), calls=%async_computation.1 | async-start | bytes 3145728 | tf_op jit(solution)/shard_map/all_gather | solution.py:91
  100.0 114.6 %all-gather.27.cloned.1.call-start = ((), (), s32[]{:S(2)}) async-start(), calls=%async_computation.5 | async-start | bytes 3145728 | tf_op jit(solution)/shard_map/all_gather | solution.py:91
  191.2 31.4 %collective-permute-start.27 = (f16[256,1792]{1,0:T(8,128)(2,1)}, f16[256,1792]{1,0:T(8,128)(2,1)}, u32[]{:S(2)}, u32[]{:S(2)}) collective-permute-start(f16[256,1792]{1,0:T(8,128)(2,1)} %fusion.31), channel_id=1, source_target_pairs={{0,8},{1,17},{8,0},{9,25},{16,24},{17,1},{24,16},{25,9},{2,10},{3,... | collective-permute-start | bytes 2752520 | tf_op jit(solution)/shard_map/ppermute | solution.py:68
  212.6 16.1 %collective-permute-start.9 = (f16[256,1792]{1,0:T(8,128)(2,1)}, f16[256,1792]{1,0:T(8,128)(2,1)S(1)}, u32[]{:S(2)}, u32[]{:S(2)}) collective-permute-start(f16[256,1792]{1,0:T(8,128)(2,1)} %fusion.28), channel_id=1, source_target_pairs={{0,8},{1,17},{8,0},{9,25},{16,24},{17,1},{24,16},{25,9},{2,10},{3,... | collective-permute-start | bytes 2752520 | tf_op jit(solution)/shard_map/ppermute | solution.py:68
  213.1 30.1 %collective-permute-start.11 = (f16[256,1792]{1,0:T(8,128)(2,1)}, f16[256,1792]{1,0:T(8,128)(2,1)S(1)}, u32[]{:S(2)}, u32[]{:S(2)}) collective-permute-start(f16[256,1792]{1,0:T(8,128)(2,1)} %fusion.29), channel_id=1, source_target_pairs={{0,8},{1,17},{8,0},{9,25},{16,24},{17,1},{24,16},{25,9},{2,10},{3,... | collective-permute-start | bytes 2752520 | tf_op jit(solution)/shard_map/ppermute | solution.py:68
  220.3 37.3 %collective-permute-start.18 = (f16[256,1792]{1,0:T(8,128)(2,1)S(1)}, f16[256,1792]{1,0:T(8,128)(2,1)S(1)}, u32[]{:S(2)}, u32[]{:S(2)}) collective-permute-start(f16[256,1792]{1,0:T(8,128)(2,1)S(1)} %fusion.30), channel_id=1, source_target_pairs={{0,8},{1,17},{8,0},{9,25},{16,24},{17,1},{24,16},{25,9},{2,10},{3,... | collective-permute-start | bytes 2752520 | tf_op jit(solution)/shard_map/ppermute | solution.py:68
  220.8 51.7 %collective-permute-start = (f16[256,1792]{1,0:T(8,128)(2,1)S(1)}, f16[256,1792]{1,0:T(8,128)(2,1)S(1)}, u32[]{:S(2)}, u32[]{:S(2)}) collective-permute-start(f16[256,1792]{1,0:T(8,128)(2,1)S(1)} %copy-done.26), channel_id=1, source_target_pairs={{0,8},{1,17},{8,0},{9,25},{16,24},{17,1},{24,16},{25,9},{2,10},{3,... | collective-permute-start | bytes 2752520 | tf_op jit(solution)/shard_map/ppermute | solution.py:68
  222.6 66.6 %collective-permute-start.2 = (f16[256,1792]{1,0:T(8,128)(2,1)S(1)}, f16[256,1792]{1,0:T(8,128)(2,1)}, u32[]{:S(2)}, u32[]{:S(2)}) collective-permute-start(f16[256,1792]{1,0:T(8,128)(2,1)S(1)} %copy-done.25), channel_id=1, source_target_pairs={{0,8},{1,17},{8,0},{9,25},{16,24},{17,1},{24,16},{25,9},{2,10},{3,... | collective-permute-start | bytes 2752520 | tf_op jit(solution)/shard_map/ppermute | solution.py:68
  228.7 65.0 %collective-permute-start.28 = (f16[128,1792]{1,0:T(8,128)(2,1)S(1)}, f16[128,1792]{1,0:T(8,128)(2,1)S(1)}, u32[]{:S(2)}, u32[]{:S(2)}) collective-permute-start(f16[128,1792]{1,0:T(8,128)(2,1)S(1)} %multiply_convert_fusion.2), channel_id=1, source_target_pairs={{0,16},{1,9},{8,24},{9,1},{16,0},{17,25},{24,8},{25,17},{2,18},{3,... | collective-permute-start | bytes 1376264 | tf_op jit(solution)/shard_map/ppermute | solution.py:68
  230.7 28.6 %slice-start.6 = ((s8[7340032]{0:T(1024)(128)(4,1)}), s8[4194304]{0:T(1024)(128)(4,1)S(1)}, s32[]{:S(2)}) async-start(s8[7340032]{0:T(1024)(128)(4,1)} %bitcast.127), calls=%async_computation.14 | async-start | bytes 8388608
  232.9 26.4 %slice-start.7 = ((s8[7340032]{0:T(1024)(128)(4,1)}), s8[3145728]{0:T(1024)(128)(4,1)S(1)}, s32[]{:S(2)}) async-start(s8[7340032]{0:T(1024)(128)(4,1)} %bitcast.127), calls=%async_computation.15 | async-start | bytes 6291456
  243.2 51.4 %collective-permute-start.10 = (f16[128,1792]{1,0:T(8,128)(2,1)S(1)}, f16[128,1792]{1,0:T(8,128)(2,1)S(1)}, u32[]{:S(2)}, u32[]{:S(2)}) collective-permute-start(f16[128,1792]{1,0:T(8,128)(2,1)S(1)} %multiply_convert_fusion.8), channel_id=1, source_target_pairs={{0,16},{1,9},{8,24},{9,1},{16,0},{17,25},{24,8},{25,17},{2,18},{3,... | collective-permute-start | bytes 1376264 | tf_op jit(solution)/shard_map/ppermute | solution.py:68
  247.6 27.2 %copy-start.23 = (bf16[4,128,2048]{2,1,0:T(8,128)(2,1)S(1)}, bf16[4,128,2048]{2,1,0:T(8,128)(2,1)}, u32[]{:S(2)}) copy-start(bf16[4,128,2048]{2,1,0:T(8,128)(2,1)} %all-gather.19.cloned.1.call-done) | copy-start | bytes 6291460
  257.6 37.0 %collective-permute-start.12 = (f16[128,1792]{1,0:T(8,128)(2,1)S(1)}, f16[128,1792]{1,0:T(8,128)(2,1)S(1)}, u32[]{:S(2)}, u32[]{:S(2)}) collective-permute-start(f16[128,1792]{1,0:T(8,128)(2,1)S(1)} %multiply_convert_fusion.7), channel_id=1, source_target_pairs={{0,16},{1,9},{8,24},{9,1},{16,0},{17,25},{24,8},{25,17},{2,18},{3,... | collective-permute-start | bytes 1376264 | tf_op jit(solution)/shard_map/ppermute | solution.py:68
  273.4 23.2 %collective-permute-start.19 = (f16[128,1792]{1,0:T(8,128)(2,1)S(1)}, f16[128,1792]{1,0:T(8,128)(2,1)S(1)}, u32[]{:S(2)}, u32[]{:S(2)}) collective-permute-start(f16[128,1792]{1,0:T(8,128)(2,1)S(1)} %multiply_convert_fusion.5), channel_id=1, source_target_pairs={{0,16},{1,9},{8,24},{9,1},{16,0},{17,25},{24,8},{25,17},{2,18},{3,... | collective-permute-start | bytes 1376264 | tf_op jit(solution)/shard_map/ppermute | solution.py:68
  289.2 8.5 %collective-permute-start.1 = (f16[128,1792]{1,0:T(8,128)(2,1)S(1)}, f16[128,1792]{1,0:T(8,128)(2,1)S(1)}, u32[]{:S(2)}, u32[]{:S(2)}) collective-permute-start(f16[128,1792]{1,0:T(8,128)(2,1)S(1)} %multiply_convert_fusion.11), channel_id=1, source_target_pairs={{0,16},{1,9},{8,24},{9,1},{16,0},{17,25},{24,8},{25,17},{2,18},{3,... | collective-permute-start | bytes 1376264 | tf_op jit(solution)/shard_map/ppermute | solution.py:68
  293.7 8.8 %collective-permute-start.3 = (f16[128,1792]{1,0:T(8,128)(2,1)S(1)}, f16[128,1792]{1,0:T(8,128)(2,1)S(1)}, u32[]{:S(2)}, u32[]{:S(2)}) collective-permute-start(f16[128,1792]{1,0:T(8,128)(2,1)S(1)} %multiply_convert_fusion.10), channel_id=1, source_target_pairs={{0,16},{1,9},{8,24},{9,1},{16,0},{17,25},{24,8},{25,17},{2,18},{3,... | collective-permute-start | bytes 1376264 | tf_op jit(solution)/shard_map/ppermute | solution.py:68
  295.4 12.5 %collective-permute-start.13 = (bf16[128,1792]{1,0:T(8,128)(2,1)S(1)}, bf16[128,1792]{1,0:T(8,128)(2,1)S(1)}, u32[]{:S(2)}, u32[]{:S(2)}) collective-permute-start(bf16[128,1792]{1,0:T(8,128)(2,1)S(1)} %get-tuple-element.16), channel_id=1, source_target_pairs={{0,16},{1,9},{8,24},{9,1},{16,0},{17,25},{24,8},{25,17},{2,18},{3,... | collective-permute-start | bytes 1376264 | tf_op jit(solution)/shard_map/ppermute | solution.py:68
  303.7 13.4 %collective-permute-start.4 = (bf16[128,1792]{1,0:T(8,128)(2,1)S(1)}, bf16[128,1792]{1,0:T(8,128)(2,1)S(1)}, u32[]{:S(2)}, u32[]{:S(2)}) collective-permute-start(bf16[128,1792]{1,0:T(8,128)(2,1)S(1)} %get-tuple-element.13), channel_id=1, source_target_pairs={{0,16},{1,9},{8,24},{9,1},{16,0},{17,25},{24,8},{25,17},{2,18},{3,... | collective-permute-start | bytes 1376264 | tf_op jit(solution)/shard_map/ppermute | solution.py:68
  305.0 22.0 %collective-permute-start.31 = (bf16[128,1792]{1,0:T(8,128)(2,1)S(1)}, bf16[128,1792]{1,0:T(8,128)(2,1)S(1)}, u32[]{:S(2)}, u32[]{:S(2)}) collective-permute-start(bf16[128,1792]{1,0:T(8,128)(2,1)S(1)} %get-tuple-element.14), channel_id=1, source_target_pairs={{0,16},{1,9},{8,24},{9,1},{16,0},{17,25},{24,8},{25,17},{2,18},{3,... | collective-permute-start | bytes 1376264 | tf_op jit(solution)/shard_map/ppermute | solution.py:68
  305.8 31.0 %collective-permute-start.29 = (bf16[128,1792]{1,0:T(8,128)(2,1)S(1)}, bf16[128,1792]{1,0:T(8,128)(2,1)S(1)}, u32[]{:S(2)}, u32[]{:S(2)}) collective-permute-start(bf16[128,1792]{1,0:T(8,128)(2,1)S(1)} %get-tuple-element.15), channel_id=1, source_target_pairs={{0,16},{1,9},{8,24},{9,1},{16,0},{17,25},{24,8},{25,17},{2,18},{3,... | collective-permute-start | bytes 1376264 | tf_op jit(solution)/shard_map/ppermute | solution.py:68
  307.0 39.6 %collective-permute-start.22 = (bf16[128,1792]{1,0:T(8,128)(2,1)S(1)}, bf16[128,1792]{1,0:T(8,128)(2,1)S(1)}, u32[]{:S(2)}, u32[]{:S(2)}) collective-permute-start(bf16[128,1792]{1,0:T(8,128)(2,1)S(1)} %get-tuple-element.11), channel_id=1, source_target_pairs={{0,16},{1,9},{8,24},{9,1},{16,0},{17,25},{24,8},{25,17},{2,18},{3,... | collective-permute-start | bytes 1376264 | tf_op jit(solution)/shard_map/ppermute | solution.py:68
  307.9 48.6 %collective-permute-start.20 = (bf16[128,1792]{1,0:T(8,128)(2,1)S(1)}, bf16[128,1792]{1,0:T(8,128)(2,1)S(1)}, u32[]{:S(2)}, u32[]{:S(2)}) collective-permute-start(bf16[128,1792]{1,0:T(8,128)(2,1)S(1)} %get-tuple-element.12), channel_id=1, source_target_pairs={{0,16},{1,9},{8,24},{9,1},{16,0},{17,25},{24,8},{25,17},{2,18},{3,... | collective-permute-start | bytes 1376264 | tf_op jit(solution)/shard_map/ppermute | solution.py:68
  317.2 43.0 %collective-permute-start.14 = (bf16[256,1792]{1,0:T(8,128)(2,1)S(1)}, bf16[256,1792]{1,0:T(8,128)(2,1)S(1)}, u32[]{:S(2)}, u32[]{:S(2)}) collective-permute-start(bf16[256,1792]{1,0:T(8,128)(2,1)S(1)} %pad_maximum_fusion.12), channel_id=1, source_target_pairs={{0,8},{1,17},{8,0},{9,25},{16,24},{17,1},{24,16},{25,9},{2,10},{3,... | collective-permute-start | bytes 2752520 | tf_op jit(solution)/shard_map/ppermute | solution.py:68
  327.0 33.6 %collective-permute-start.5 = (bf16[256,1792]{1,0:T(8,128)(2,1)S(1)}, bf16[256,1792]{1,0:T(8,128)(2,1)S(1)}, u32[]{:S(2)}, u32[]{:S(2)}) collective-permute-start(bf16[256,1792]{1,0:T(8,128)(2,1)S(1)} %pad_maximum_fusion.11), channel_id=1, source_target_pairs={{0,8},{1,17},{8,0},{9,25},{16,24},{17,1},{24,16},{25,9},{2,10},{3,... | collective-permute-start | bytes 2752520 | tf_op jit(solution)/shard_map/ppermute | solution.py:68
  336.8 33.9 %collective-permute-start.32 = (bf16[256,1792]{1,0:T(8,128)(2,1)S(1)}, bf16[256,1792]{1,0:T(8,128)(2,1)}, u32[]{:S(2)}, u32[]{:S(2)}) collective-permute-start(bf16[256,1792]{1,0:T(8,128)(2,1)S(1)} %pad_maximum_fusion.16), channel_id=1, source_target_pairs={{0,8},{1,17},{8,0},{9,25},{16,24},{17,1},{24,16},{25,9},{2,10},{3,... | collective-permute-start | bytes 2752520 | tf_op jit(solution)/shard_map/ppermute | solution.py:68
  346.7 26.3 %collective-permute-start.30 = (bf16[256,1792]{1,0:T(8,128)(2,1)}, bf16[256,1792]{1,0:T(8,128)(2,1)}, u32[]{:S(2)}, u32[]{:S(2)}) collective-permute-start(bf16[256,1792]{1,0:T(8,128)(2,1)} %pad_maximum_fusion.15), channel_id=1, source_target_pairs={{0,8},{1,17},{8,0},{9,25},{16,24},{17,1},{24,16},{25,9},{2,10},{3,... | collective-permute-start | bytes 2752520 | tf_op jit(solution)/shard_map/ppermute | solution.py:68
  356.5 25.6 %collective-permute-start.23 = (bf16[256,1792]{1,0:T(8,128)(2,1)}, bf16[256,1792]{1,0:T(8,128)(2,1)}, u32[]{:S(2)}, u32[]{:S(2)}) collective-permute-start(bf16[256,1792]{1,0:T(8,128)(2,1)} %pad_maximum_fusion.14), channel_id=1, source_target_pairs={{0,8},{1,17},{8,0},{9,25},{16,24},{17,1},{24,16},{25,9},{2,10},{3,... | collective-permute-start | bytes 2752520 | tf_op jit(solution)/shard_map/ppermute | solution.py:68
  360.2 23.6 %collective-permute-start.21 = (bf16[256,1792]{1,0:T(8,128)(2,1)}, bf16[256,1792]{1,0:T(8,128)(2,1)}, u32[]{:S(2)}, u32[]{:S(2)}) collective-permute-start(bf16[256,1792]{1,0:T(8,128)(2,1)} %pad_maximum_fusion.13), channel_id=1, source_target_pairs={{0,8},{1,17},{8,0},{9,25},{16,24},{17,1},{24,16},{25,9},{2,10},{3,... | collective-permute-start | bytes 2752520 | tf_op jit(solution)/shard_map/ppermute | solution.py:68
  367.4 91.2 %collective-permute-start.15 = (f32[256,2048]{1,0:T(8,128)}, f32[256,2048]{1,0:T(8,128)}, u32[]{:S(2)}, u32[]{:S(2)}) collective-permute-start(f32[256,2048]{1,0:T(8,128)} %fusion.99), channel_id=1, source_target_pairs={{0,1},{1,0},{2,3},{3,2},{4,5},{5,4},{6,7},{7,6},{8,9},{9,8},{10,11... | collective-permute-start | bytes 6291464 | tf_op jit(solution)/shard_map/ppermute | solution.py:107
  370.8 92.8 %collective-permute-start.6 = (f32[256,2048]{1,0:T(8,128)}, f32[256,2048]{1,0:T(8,128)}, u32[]{:S(2)}, u32[]{:S(2)}) collective-permute-start(f32[256,2048]{1,0:T(8,128)} %fusion.98), channel_id=1, source_target_pairs={{0,1},{1,0},{2,3},{3,2},{4,5},{5,4},{6,7},{7,6},{8,9},{9,8},{10,11... | collective-permute-start | bytes 6291464 | tf_op jit(solution)/shard_map/ppermute | solution.py:107
  382.1 86.4 %collective-permute-start.33 = (f32[256,2048]{1,0:T(8,128)}, f32[256,2048]{1,0:T(8,128)}, u32[]{:S(2)}, u32[]{:S(2)}) collective-permute-start(f32[256,2048]{1,0:T(8,128)} %convolution_add_fusion), channel_id=1, source_target_pairs={{0,1},{1,0},{2,3},{3,2},{4,5},{5,4},{6,7},{7,6},{8,9},{9,8},{10,11... | collective-permute-start | bytes 6291464 | tf_op jit(solution)/shard_map/ppermute | solution.py:107
  393.3 80.3 %collective-permute-start.24 = (f32[256,2048]{1,0:T(8,128)}, f32[256,2048]{1,0:T(8,128)}, u32[]{:S(2)}, u32[]{:S(2)}) collective-permute-start(f32[256,2048]{1,0:T(8,128)} %convolution_add_fusion.2), channel_id=1, source_target_pairs={{0,1},{1,0},{2,3},{3,2},{4,5},{5,4},{6,7},{7,6},{8,9},{9,8},{10,11... | collective-permute-start | bytes 6291464 | tf_op jit(solution)/shard_map/ppermute | solution.py:107
  462.5 16.2 %collective-permute-start.16 = (bf16[128,2048]{1,0:T(8,128)(2,1)S(1)}, bf16[128,2048]{1,0:T(8,128)(2,1)S(1)}, u32[]{:S(2)}, u32[]{:S(2)}) collective-permute-start(bf16[128,2048]{1,0:T(8,128)(2,1)S(1)} %bitcast.174), channel_id=1, source_target_pairs={{0,2},{2,0},{4,6},{6,4},{1,3},{3,1},{5,7},{7,5},{8,10},{10,8},{12,... | collective-permute-start | bytes 1572872 | tf_op jit(solution)/shard_map/ppermute | solution.py:120
  467.5 26.7 %collective-permute-start.7 = (bf16[128,2048]{1,0:T(8,128)(2,1)S(1)}, bf16[128,2048]{1,0:T(8,128)(2,1)S(1)}, u32[]{:S(2)}, u32[]{:S(2)}) collective-permute-start(bf16[128,2048]{1,0:T(8,128)(2,1)S(1)} %bitcast.175), channel_id=1, source_target_pairs={{0,2},{2,0},{4,6},{6,4},{1,3},{3,1},{5,7},{7,5},{8,10},{10,8},{12,... | collective-permute-start | bytes 1572872 | tf_op jit(solution)/shard_map/ppermute | solution.py:120
  472.4 38.7 %collective-permute-start.34 = (bf16[128,2048]{1,0:T(8,128)(2,1)S(1)}, bf16[128,2048]{1,0:T(8,128)(2,1)S(1)}, u32[]{:S(2)}, u32[]{:S(2)}) collective-permute-start(bf16[128,2048]{1,0:T(8,128)(2,1)S(1)} %bitcast.176), channel_id=1, source_target_pairs={{0,2},{2,0},{4,6},{6,4},{1,3},{3,1},{5,7},{7,5},{8,10},{10,8},{12,... | collective-permute-start | bytes 1572872 | tf_op jit(solution)/shard_map/ppermute | solution.py:120
  477.5 44.0 %collective-permute-start.25 = (bf16[128,2048]{1,0:T(8,128)(2,1)S(1)}, bf16[128,2048]{1,0:T(8,128)(2,1)S(1)}, u32[]{:S(2)}, u32[]{:S(2)}) collective-permute-start(bf16[128,2048]{1,0:T(8,128)(2,1)S(1)} %bitcast.177), channel_id=1, source_target_pairs={{0,2},{2,0},{4,6},{6,4},{1,3},{3,1},{5,7},{7,5},{8,10},{10,8},{12,... | collective-permute-start | bytes 1572872 | tf_op jit(solution)/shard_map/ppermute | solution.py:120
  478.8 44.3 %collective-permute-start.17 = (bf16[64,2048]{1,0:T(8,128)(2,1)S(1)}, bf16[64,2048]{1,0:T(8,128)(2,1)S(1)}, u32[]{:S(2)}, u32[]{:S(2)}) collective-permute-start(bf16[64,2048]{1,0:T(8,128)(2,1)S(1)} %fusion.68), channel_id=1, source_target_pairs={{0,4},{2,6},{4,0},{6,2},{1,5},{3,7},{5,1},{7,3},{8,12},{10,14},{12... | collective-permute-start | bytes 786440 | tf_op jit(solution)/shard_map/ppermute | solution.py:120
  494.4 28.8 %collective-permute-start.8 = (bf16[64,2048]{1,0:T(8,128)(2,1)S(1)}, bf16[64,2048]{1,0:T(8,128)(2,1)S(1)}, u32[]{:S(2)}, u32[]{:S(2)}) collective-permute-start(bf16[64,2048]{1,0:T(8,128)(2,1)S(1)} %fusion.67), channel_id=1, source_target_pairs={{0,4},{2,6},{4,0},{6,2},{1,5},{3,7},{5,1},{7,3},{8,12},{10,14},{12... | collective-permute-start | bytes 786440 | tf_op jit(solution)/shard_map/ppermute | solution.py:120
  511.2 28.9 %collective-permute-start.35 = (bf16[64,2048]{1,0:T(8,128)(2,1)S(1)}, bf16[64,2048]{1,0:T(8,128)(2,1)S(1)}, u32[]{:S(2)}, u32[]{:S(2)}) collective-permute-start(bf16[64,2048]{1,0:T(8,128)(2,1)S(1)} %fusion.70), channel_id=1, source_target_pairs={{0,4},{2,6},{4,0},{6,2},{1,5},{3,7},{5,1},{7,3},{8,12},{10,14},{12... | collective-permute-start | bytes 786440 | tf_op jit(solution)/shard_map/ppermute | solution.py:120
  521.7 23.9 %collective-permute-start.26 = (bf16[64,2048]{1,0:T(8,128)(2,1)S(1)}, bf16[64,2048]{1,0:T(8,128)(2,1)S(1)}, u32[]{:S(2)}, u32[]{:S(2)}) collective-permute-start(bf16[64,2048]{1,0:T(8,128)(2,1)S(1)} %fusion.69), channel_id=1, source_target_pairs={{0,4},{2,6},{4,0},{6,2},{1,5},{3,7},{5,1},{7,3},{8,12},{10,14},{12... | collective-permute-start | bytes 786440 | tf_op jit(solution)/shard_map/ppermute | solution.py:120
  (37 other events, 279.4 us)
Sparse Core Ops, SparseCore 0:
  10.1 30.6 all-gather.28
  42.9 27.4 all-gather.20
  72.6 27.4 all-gather.16
  102.0 27.4 all-gather.24
  130.9 10.0 all-gather.30
  142.4 11.7 all-gather.22
  155.7 11.7 all-gather.18
  184.9 9.9 all-gather.26

commit v2 on v1

--- a/solution.py
+++ b/solution.py
@@ -86,16 +86,41 @@
         return values
 
 
+def after(values, earlier):
+    return lax.optimization_barrier((values, earlier))[0]
+
+
+def swap_cores(values):
+    return lax.ppermute(values, "depth", [(0, 1), (1, 0)])
+
+
 def gather_tokens(values):
-    over_col = lax.all_gather(values, "col", axis=0)
-    both = lax.all_gather(over_col, "depth", axis=1)
-    return both.reshape(-1, values.shape[1])
-
-
-def scatter_tokens(term):
+    cols, cores = lax.axis_size("col"), lax.axis_size("depth")
+    assert cores == 2 and cols & (cols - 1) == 0
+    me = lax.axis_index("col")
+    blocks = [values[None]]
+    for other in range(1, cols):
+        pairs = [(c, c ^ other) for c in range(cols)]
+        blocks.append(lax.ppermute(values, "col", pairs)[None])
+    bit = 0
+    while len(blocks) > 1:
+        side = (me >> bit) & 1
+        blocks = [
+            join_halves(blocks[k], blocks[k + 1], side) for k in range(0, len(blocks), 2)
+        ]
+        bit += 1
+    mine = blocks[0]
+    other = swap_cores(mine)
+    core = lax.axis_index("depth")
+    first = jnp.where(core == 0, mine, other)
+    second = jnp.where(core == 0, other, mine)
+    return jnp.stack([first, second], axis=1).reshape(-1, values.shape[1])
+
+
+def core_sum(term):
     cols, cores = lax.axis_size("col"), lax.axis_size("depth")
     assert cores == 2
-    core, me = lax.axis_index("depth"), lax.axis_index("col")
+    core = lax.axis_index("depth")
 
     def rows_of(which):
         def select(values):
@@ -104,22 +129,25 @@
 
         return select
 
-    landed = lax.ppermute(term(rows_of(1 - core)), "depth", [(0, 1), (1, 0)])
-    total = term(rows_of(core)) + landed
-    width = total.shape[1]
-    bits = cols.bit_length() - 1
-    assert 1 << bits == cols
-    for bit in range(bits):
-        side = (me >> bit) & 1
-        shaped = total.reshape(cols >> (bit + 1), 2, -1, width)
-
-        def pick(which):
-            return lax.dynamic_index_in_dim(shaped, which, 1, keepdims=False).reshape(-1, width)
-
-        pairs = [(c, c ^ (1 << bit)) for c in range(cols)]
-        landed = lax.ppermute(pick(1 - side).astype(BF16), "col", pairs)
-        total = pick(side) + landed.astype(F32)
-    return total
+    landed = swap_cores(term(rows_of(1 - core)))
+    return term(rows_of(core)) + landed
+
+
+def col_stage(total, bit):
+    cols, width = lax.axis_size("col"), total.shape[1]
+    assert cols & (cols - 1) == 0
+    side = (lax.axis_index("col") >> bit) & 1
+    shaped = total.reshape(cols >> (bit + 1), 2, -1, width)
+
+    def pick(which):
+        return lax.dynamic_index_in_dim(shaped, which, 1, keepdims=False).reshape(-1, width)
+
+    return pick(side), pick(1 - side).astype(BF16)
+
+
+def col_swap(kept, sent, bit):
+    pairs = [(c, c ^ (1 << bit)) for c in range(lax.axis_size("col"))]
+    return kept + lax.ppermute(sent, "col", pairs).astype(F32)
 
 
 def product_bounds(tokens, out_grad, gate_weight, up_weight, down_weight):
@@ -138,9 +166,12 @@
     row = RowGroup()
     own = tokens.shape[0] // SPLIT
     inputs, grads_in = [], []
+    last = None
     for part in range(SPLIT):
-        inputs.append(gather_tokens(tokens[part * own : (part + 1) * own]))
-        grads_in.append(gather_tokens(out_grad[part * own : (part + 1) * own]))
+        for source, gathered in ((tokens, inputs), (out_grad, grads_in)):
+            rows = source[part * own : (part + 1) * own]
+            last = gather_tokens(rows if last is None else after(rows, last))
+            gathered.append(last)
     gate_bound, up_bound, hidden_bound = product_bounds(
         tokens, out_grad, gate_weight, up_weight, down_weight
     )
@@ -168,9 +199,9 @@
         hidden_grad = row.scatter_product(grads_in[part], w_down, hidden_bound)
         gate_term = row.gather((hidden_grad * up * sig * (1.0 + gate * (1.0 - sig))).astype(BF16))
         up_term = row.gather((hidden_grad * act).astype(BF16))
-        outputs.append(scatter_tokens(lambda select: contract_last(select(hidden), w_down)))
+        outputs.append(core_sum(lambda select: contract_last(select(hidden), w_down)))
         in_grads.append(
-            scatter_tokens(
+            core_sum(
                 lambda select: contract_last(select(gate_term), w_gate)
                 + contract_last(select(up_term), w_up)
             )
@@ -183,10 +214,22 @@
         return jnp.concatenate(parts, axis=0)
 
     all_inputs, all_grads = joined(inputs), joined(grads_in)
-    gate_grad = contract_first(all_inputs, joined(gate_terms)) * full_gate.astype(F32)
-    up_grad = contract_first(all_inputs, joined(up_terms)) * full_up.astype(F32)
     down_grad = contract_first(all_grads, joined(hiddens)) * full_down.astype(F32)
-    return (joined(outputs), joined(in_grads), gate_grad, up_grad, down_grad)
+    lefts, weight_grads = [all_inputs, all_inputs], []
+    rights = [(gate_terms, full_gate), (up_terms, full_up)]
+    sums = outputs + in_grads
+    for bit in range(lax.axis_size("col").bit_length() - 1):
+        staged = [col_stage(total, bit) for total in sums]
+        if lefts:
+            sent, left = lax.optimization_barrier(([s for _, s in staged], lefts.pop()))
+            staged = [(kept, s) for (kept, _), s in zip(staged, sent)]
+            terms, mask = rights[len(weight_grads)]
+            weight_grads.append(contract_first(left, joined(terms)) * mask.astype(F32))
+        sums = [col_swap(kept, s, bit) for kept, s in staged]
+    for terms, mask in rights[len(weight_grads) :]:
+        weight_grads.append(contract_first(all_inputs, joined(terms)) * mask.astype(F32))
+    gate_grad, up_grad = weight_grads
+    return (joined(sums[:SPLIT]), joined(sums[SPLIT:]), gate_grad, up_grad, down_grad)
 
 
 def solution(mesh):

time: 561 us -> 501 us (0.89)
  waiting for transfers between devices: 229 us -> 149 us
  other arithmetic: 42.2 us -> 64.5 us
  local copies, waits for them, and re-layouts: 25.5 us -> 44.7 us
  matrix products: 144 us -> 127 us
  between operations: 19.2 us -> 6.5 us
    all_gather x8 -> x0, waiting for transfers between devices: 87.5 us -> none  [the longest x4 87.5 us: gather_tokens(): over_col = lax.all_gather(values, 'col', axis=0)]
    ppermute x12 -> x28, waiting for transfers between devices: 57.9 us -> 84.2 us  [the longest x8 50.7 us: col_swap(): return kept + lax.ppermute(sent, 'col', pairs).astype(F32)]
    ppermute x24, waiting for transfers between devices: 82.6 us -> 64.8 us  [swap(): return lax.ppermute(values, ('row', 'depth'), pairs)]
    dot_general x6, matrix products: 31.2 us -> 15.2 us  [scatter_product(): away = jnp.dot(half_at(left, 1 - bit), right, preferred_element_type=F32)]
    ppermute x12 -> x28, starting transfers between devices: 18.6 us -> 30.8 us  [the longest x12 19.6 us: gather_tokens(): blocks.append(lax.ppermute(values, 'col', pairs)[None])]
    dot_general x12, matrix products: 44.9 us -> 56.2 us  [contract_last(): lax.dot_general(left, right, (((1,), (1,)), ((), ())), preferred_element_...]
    convert_element_type x8, local copies, waits for them, and re-layouts: 0.43 us -> 9.15 us  [col_stage(): return (pick(side), pick(1 - side).astype(BF16))]
    dot_general x3, matrix products: 47.8 us -> 39.3 us  [contract_first(): lax.dot_general(left, right, (((0,), (0,)), ((), ())), preferred_element_...]
  transfers between devices with their start and end apart: 44 -> 52, of which waited for: 19 -> 22; matrix products, arithmetic and copies ran while one was open for 37% -> 43% of each run, Pallas kernels for 0% -> 0%
where the time goes in v2:
time: 501 us; the launch traced here: 493 us
  waiting for transfers between devices  149 us (30%)
  matrix products  127 us (25%)
  other arithmetic  64.5 us (13%)
  starting transfers between devices  57.8 us (12%)
  local copies, waits for them, and re-layouts  44.7 us (9%)
  blocking collectives  43.8 us (9%)
  between operations  6.5 us (1%)
    ppermute x24, waiting for transfers between devices, swap(): return lax.ppermute(values, ('row', 'depth'), pairs)  64.8 us
    dot_general x12, matrix products, contract_last(): lax.dot_general(left, right, (((1,), (1,)), ((), ())), preferred_element_...  56.2 us
    ppermute x8, waiting for transfers between devices, col_swap(): return kept + lax.ppermute(sent, 'col', pairs).astype(F32)  50.7 us
    pmax x1, blocking collectives, product_bounds(): tops = lax.pmax(jnp.stack(tops), ('row', 'col', 'depth'))  43.8 us
    dot_general x3, matrix products, contract_first(): lax.dot_general(left, right, (((0,), (0,)), ((), ())), preferred_element_...  39.3 us
    ppermute x12, waiting for transfers between devices, gather_tokens(): blocks.append(lax.ppermute(values, 'col', pairs)[None])  33.5 us
    ppermute x24, starting transfers between devices, swap(): return lax.ppermute(values, ('row', 'depth'), pairs)  26.9 us
    ppermute x12, starting transfers between devices, gather_tokens(): blocks.append(lax.ppermute(values, 'col', pairs)[None])  19.6 us
  transfers between devices with their start and end apart: 52, of which 22 were waited for; matrix products, arithmetic and copies ran while one was open for 43% of the time, Pallas kernels for 0%

profile of v2, /device:TPU:0, one launch (start us, length us, event | category | flops | bytes accessed | tf_op | source)
XLA Modules:
  0.0 493.3 jit_solution(621580601999627682)
XLA Ops:
  2.3 3.0 collective-permute-start
  9.0 9.1 %bitcast_multiply_fusion = (bf16[2048,1792]{1,0:T(8,128)(2,1)}, bf16[]{:T(256)}) fusion(bf16[2048,1792]{1,0:T(8,128)(2,1)} %param.12, bf16[32,1792]{1,0:T(8,128)(2,1)S(1)} %fusion.34), kind=kLoop, calls=%fused_computation.31 | loop fusion | flops 11010047 | bytes 14794754 | tf_op jit(solution)/shard_map/mul | solution.py:30
  18.3 5.9 %bitcast_multiply_fusion.2 = (bf16[2048,1792]{1,0:T(8,128)(2,1)}, bf16[]{:T(256)}) fusion(bf16[2048,1792]{1,0:T(8,128)(2,1)S(1)} %bitcast.180, bf16[32,1792]{1,0:T(8,128)(2,1)S(1)} %fusion.32), kind=kLoop, calls=%fused_computation.33 | loop fusion | flops 11010047 | bytes 14794754 | tf_op jit(solution)/shard_map/mul | solution.py:30
  30.3 9.1 %abs_reduce_fusion.1 = (bf16[]{:T(256)}, bf16[2048,1792]{1,0:T(8,128)(2,1)}) fusion(bf16[2048,1792]{1,0:T(8,128)(2,1)} %param.11, bf16[32,1792]{1,0:T(8,128)(2,1)S(1)} %fusion.33), kind=kLoop, calls=%fused_computation.4 | loop fusion | flops 11010047 | bytes 14794754 | tf_op jit(solution)/shard_map/reduce_max | solution.py:154
  40.9 3.3 stack.70
  44.2 43.8 %pmax.7 = f32[5]{0:T(128)S(1)} all-reduce(bf16[5]{0:T(256)(128)(2,1)S(1)} %stack.70), channel_id=1, replica_groups=mesh['row'=4,'col'=4,'depth'=2] {'row','col','depth'}, use_global_device_ids=true, to_apply=%region_5.6 | all-reduce | flops 5 | bytes 30 | tf_op jit(solution)/shard_map/pmax | solution.py:155
  92.8 3.4 mul.261
  96.2 3.5 mul.278
  99.7 3.5 mul.292
  117.2 10.3 %collective-permute-done.11 = bf16[64,2048]{1,0:T(8,128)(2,1)S(1)} collective-permute-done((bf16[64,2048]{1,0:T(8,128)(2,1)S(1)}, bf16[64,2048]{1,0:T(8,128)(2,1)S(1)}, u32[]{:S(2)}, u32[]{:S(2)}) %collective-permute-start.11) | collective-permute-done | bytes 262176 | tf_op jit(solution)/shard_map/ppermute | solution.py:104
  132.4 5.9 %collective-permute-done.6 = f16[256,1792]{1,0:T(8,128)(2,1)S(1)} collective-permute-done((f16[256,1792]{1,0:T(8,128)(2,1)S(1)}, f16[256,1792]{1,0:T(8,128)(2,1)S(1)}, u32[]{:S(2)}, u32[]{:S(2)}) %collective-permute-start.6) | collective-permute-done | bytes 917536 | tf_op jit(solution)/shard_map/ppermute | solution.py:68
  141.1 2.7 collective-permute-start.17
  149.2 10.0 %collective-permute-done.15 = bf16[64,2048]{1,0:T(8,128)(2,1)S(1)} collective-permute-done((bf16[64,2048]{1,0:T(8,128)(2,1)S(1)}, bf16[64,2048]{1,0:T(8,128)(2,1)S(1)}, u32[]{:S(2)}, u32[]{:S(2)}) %collective-permute-start.15) | collective-permute-done | bytes 262176 | tf_op jit(solution)/shard_map/ppermute | solution.py:104
  166.5 4.9 collective-permute-start.34
  173.3 3.0 fusion.28
  176.3 3.0 fusion.29
  184.3 10.5 %collective-permute-done.33 = bf16[64,2048]{1,0:T(8,128)(2,1)S(1)} collective-permute-done((bf16[64,2048]{1,0:T(8,128)(2,1)}, bf16[64,2048]{1,0:T(8,128)(2,1)S(1)}, u32[]{:S(2)}, u32[]{:S(2)}) %collective-permute-start.33) | collective-permute-done | bytes 262176 | tf_op jit(solution)/shard_map/ppermute | solution.py:104
  200.6 6.2 %collective-permute-done.8 = bf16[128,1792]{1,0:T(8,128)(2,1)S(1)} collective-permute-done((bf16[128,1792]{1,0:T(8,128)(2,1)S(1)}, bf16[128,1792]{1,0:T(8,128)(2,1)S(1)}, u32[]{:S(2)}, u32[]{:S(2)}) %collective-permute-start.8) | collective-permute-done | bytes 458784 | tf_op jit(solution)/shard_map/ppermute | solution.py:68
  208.6 3.2 collective-permute-done.30
  212.6 4.4 collective-permute-done.28
  224.8 3.3 multiply_add_fusion.2
  230.6 3.0 fusion.31
  233.6 12.5 %collective-permute-done.31 = bf16[256,1792]{1,0:T(8,128)(2,1)S(1)} collective-permute-done((bf16[256,1792]{1,0:T(8,128)(2,1)S(1)}, bf16[256,1792]{1,0:T(8,128)(2,1)S(1)}, u32[]{:S(2)}, u32[]{:S(2)}) %collective-permute-start.31) | collective-permute-done | bytes 917536 | tf_op jit(solution)/shard_map/ppermute | solution.py:68
  247.3 10.4 %collective-permute-done.29 = bf16[256,1792]{1,0:T(8,128)(2,1)} collective-permute-done((bf16[256,1792]{1,0:T(8,128)(2,1)S(1)}, bf16[256,1792]{1,0:T(8,128)(2,1)}, u32[]{:S(2)}, u32[]{:S(2)}) %collective-permute-start.29) | collective-permute-done | bytes 917536 | tf_op jit(solution)/shard_map/ppermute | solution.py:68
  263.7 6.6 %convolution_add_fusion.2 = f32[256,2048]{1,0:T(8,128)} fusion(f32[256,2048]{1,0:T(8,128)S(1)} %fusion.100, bf16[256,1792]{1,0:T(8,128)(2,1)S(1)} %bitcast.237, bf16[2048,1792]{1,0:T(8,128)(2,1)} %get-tuple-element.36), kind=kOutput, calls=%fused_computation.42 | convolution fusion | flops 1879572480 | bytes 12451840 | tf_op jit(solution)/shard_map/dot_general | solution.py:14
  270.4 3.2 multiply_add_fusion
  275.3 3.4 fusion.99
  278.7 3.6 collective-permute-done.38
  289.3 3.2 collective-permute-done.23
  293.5 7.2 %collective-permute-done.41 = bf16[128,1792]{1,0:T(8,128)(2,1)S(1)} collective-permute-done((bf16[128,1792]{1,0:T(8,128)(2,1)S(1)}, bf16[128,1792]{1,0:T(8,128)(2,1)S(1)}, u32[]{:S(2)}, u32[]{:S(2)}) %collective-permute-start.41) | collective-permute-done | bytes 458784 | tf_op jit(solution)/shard_map/ppermute | solution.py:68
  302.5 8.1 %collective-permute-done.39 = bf16[128,1792]{1,0:T(8,128)(2,1)S(1)} collective-permute-done((bf16[128,1792]{1,0:T(8,128)(2,1)S(1)}, bf16[128,1792]{1,0:T(8,128)(2,1)S(1)}, u32[]{:S(2)}, u32[]{:S(2)}) %collective-permute-start.39) | collective-permute-done | bytes 458784 | tf_op jit(solution)/shard_map/ppermute | solution.py:68
  312.3 7.9 %fusion.24 = f32[256,2048]{1,0:T(8,128)} fusion(f32[256,2048]{1,0:T(8,128)} %collective-permute-done.32, f32[256,2048]{1,0:T(8,128)} %fusion.99, bf16[256,1792]{1,0:T(8,128)(2,1)S(1)} %bitcast.228, bf16[2048,1792]{1,0:T(8,128)(2,1)} %get-tuple-element.36), kind=kOutput, calls=%fused_computation.46 | convolution fusion | flops 1880096768 | bytes 14548992 | tf_op jit(solution)/shard_map/dot_general | solution.py:14
  328.0 3.4 fusion.97
  331.4 3.5 fusion.98
  343.8 6.5 %convolution_add_fusion = f32[256,2048]{1,0:T(8,128)} fusion(f32[256,2048]{1,0:T(8,128)S(1)} %fusion.102, bf16[256,1792]{1,0:T(8,128)(2,1)S(1)} %bitcast.235, bf16[2048,1792]{1,0:T(8,128)(2,1)} %get-tuple-element.36), kind=kOutput, calls=%fused_computation.40 | convolution fusion | flops 1879572480 | bytes 12451840 | tf_op jit(solution)/shard_map/dot_general | solution.py:14
  350.3 16.3 %convert_multiply_fusion = f32[2048,1792]{1,0:T(8,128)} fusion(bf16[2048,1792]{1,0:T(8,128)(2,1)} %bitcast.199, bf16[512,2048]{1,0:T(8,128)(2,1)} %bitcast.218, bf16[512,2048]{1,0:T(8,128)(2,1)} %bitcast.216, bf16[256,1792]{1,0:T(8,128)(2,1)} %copy-done.21, bf16[256,1792]{1,0:T(8,128)(2,1)} %copy-done.20, bf16[256,1792]{1,0:T(8,128)(2,1)} %copy-done.15, ...), kind=kOutput, calls=%fused_computation | convolution fusion | flops 7546601472 | bytes 29884416 | tf_op jit(solution)/shard_map/dot_general | solution.py:18
  366.7 6.9 %fusion.101 = f32[256,2048]{1,0:T(8,128)} fusion(bf16[256,1792]{1,0:T(8,128)(2,1)} %bitcast.233, bf16[2048,1792]{1,0:T(8,128)(2,1)} %get-tuple-element.33), kind=kOutput, calls=%fused_computation.265 | convolution fusion | flops 1879048192 | bytes 10354688 | tf_op jit(solution)/shard_map/dot_general | solution.py:14
  373.6 3.8 convolution_add_fusion.5
  378.9 3.8 convolution_add_fusion.4
  383.8 6.1 %fusion.25 = f32[256,2048]{1,0:T(8,128)} fusion(f32[256,2048]{1,0:T(8,128)} %collective-permute-done.43, f32[256,2048]{1,0:T(8,128)} %fusion.101, bf16[256,1792]{1,0:T(8,128)(2,1)} %bitcast.231, bf16[2048,1792]{1,0:T(8,128)(2,1)S(1)} %bitcast.192), kind=kOutput, calls=%fused_computation.47 | convolution fusion | flops 1880096768 | bytes 14548992 | tf_op jit(solution)/shard_map/dot_general | solution.py:14
  396.1 11.6 %convert_multiply_fusion.2 = f32[2048,1792]{1,0:T(8,128)} fusion(bf16[2048,1792]{1,0:T(8,128)(2,1)S(1)} %bitcast.198, bf16[1024,2048]{1,0:T(8,128)(2,1)S(1)} %pad_maximum_fusion, bf16[256,1792]{1,0:T(8,128)(2,1)S(1)} %copy-done.19, bf16[256,1792]{1,0:T(8,128)(2,1)S(1)} %copy-done.17, bf16[256,1792]{1,0:T(8,128)(2,1)S(1)} %copy-done.9, ...), kind=kOutput, calls=%fused_computation.2 | convolution fusion | flops 7538212864 | bytes 29884416 | tf_op jit(solution)/shard_map/dot_general | solution.py:18
  413.2 5.0 %collective-permute-done.45 = bf16[128,2048]{1,0:T(8,128)(2,1)} collective-permute-done((bf16[128,2048]{1,0:T(8,128)(2,1)}, bf16[128,2048]{1,0:T(8,128)(2,1)}, u32[]{:S(2)}, u32[]{:S(2)}) %collective-permute-start.45) | collective-permute-done | bytes 524320 | tf_op jit(solution)/shard_map/ppermute | solution.py:150
  419.4 9.9 %collective-permute-done.46 = bf16[128,2048]{1,0:T(8,128)(2,1)S(1)} collective-permute-done((bf16[128,2048]{1,0:T(8,128)(2,1)}, bf16[128,2048]{1,0:T(8,128)(2,1)S(1)}, u32[]{:S(2)}, u32[]{:S(2)}) %collective-permute-start.46) | collective-permute-done | bytes 524320 | tf_op jit(solution)/shard_map/ppermute | solution.py:150
  431.7 8.6 %collective-permute-done.47 = bf16[128,2048]{1,0:T(8,128)(2,1)} collective-permute-done((bf16[128,2048]{1,0:T(8,128)(2,1)}, bf16[128,2048]{1,0:T(8,128)(2,1)}, u32[]{:S(2)}, u32[]{:S(2)}) %collective-permute-start.47) | collective-permute-done | bytes 524320 | tf_op jit(solution)/shard_map/ppermute | solution.py:150
  449.2 11.4 %convert_multiply_fusion.1 = f32[2048,1792]{1,0:T(8,128)} fusion(bf16[2048,1792]{1,0:T(8,128)(2,1)S(1)} %bitcast.195, bf16[1024,2048]{1,0:T(8,128)(2,1)S(1)} %pad_maximum_fusion, bf16[256,1792]{1,0:T(8,128)(2,1)S(1)} %copy-done.13, bf16[256,1792]{1,0:T(8,128)(2,1)S(1)} %copy-done.11, bf16[256,1792]{1,0:T(8,128)(2,1)S(1)} %copy-done.5, ...), kind=kOutput, calls=%fused_computation.1 | convolution fusion | flops 7538212864 | bytes 29884416 | tf_op jit(solution)/shard_map/dot_general | solution.py:18
  460.5 15.6 %collective-permute-done.49 = bf16[64,2048]{1,0:T(8,128)(2,1)} collective-permute-done((bf16[64,2048]{1,0:T(8,128)(2,1)}, bf16[64,2048]{1,0:T(8,128)(2,1)}, u32[]{:S(2)}, u32[]{:S(2)}) %collective-permute-start.49) | collective-permute-done | bytes 262176 | tf_op jit(solution)/shard_map/ppermute | solution.py:150
  477.2 4.6 collective-permute-done.48
  482.8 4.6 collective-permute-done.51
  (338 shorter events, 143.8 us)
Async XLA Ops:
  2.3 21.9 %collective-permute-start = (bf16[64,2048]{1,0:T(8,128)(2,1)}, bf16[64,2048]{1,0:T(8,128)(2,1)}, u32[]{:S(2)}, u32[]{:S(2)}) collective-permute-start(bf16[64,2048]{1,0:T(8,128)(2,1)} %slice.28), channel_id=1, source_target_pairs={{0,2},{2,0},{4,6},{6,4},{1,3},{3,1},{5,7},{7,5},{8,10},{10,8},{12,... | collective-permute-start | bytes 786440 | tf_op jit(solution)/shard_map/ppermute | solution.py:104
  5.3 21.7 %collective-permute-start.1 = (bf16[64,2048]{1,0:T(8,128)(2,1)}, bf16[64,2048]{1,0:T(8,128)(2,1)}, u32[]{:S(2)}, u32[]{:S(2)}) collective-permute-start(bf16[64,2048]{1,0:T(8,128)(2,1)} %slice.28), channel_id=1, source_target_pairs={{0,4},{2,6},{4,0},{6,2},{1,5},{3,7},{5,1},{7,3},{8,12},{10,14},{12... | collective-permute-start | bytes 786440 | tf_op jit(solution)/shard_map/ppermute | solution.py:104
  7.9 19.1 %collective-permute-start.2 = (bf16[64,2048]{1,0:T(8,128)(2,1)}, bf16[64,2048]{1,0:T(8,128)(2,1)}, u32[]{:S(2)}, u32[]{:S(2)}) collective-permute-start(bf16[64,2048]{1,0:T(8,128)(2,1)} %slice.28), channel_id=1, source_target_pairs={{0,6},{2,4},{4,2},{6,0},{1,7},{3,5},{5,3},{7,1},{8,14},{10,12},{12... | collective-permute-start | bytes 786440 | tf_op jit(solution)/shard_map/ppermute | solution.py:104
  30.1 75.0 %collective-permute-start.3 = (bf16[4,64,2048]{2,1,0:T(8,128)(2,1)}, bf16[4,64,2048]{2,1,0:T(8,128)(2,1)}, u32[]{:S(2)}, u32[]{:S(2)}) collective-permute-start(bf16[4,64,2048]{2,1,0:T(8,128)(2,1)} %pad_maximum_fusion.11), channel_id=1, source_target_pairs={{0,1},{1,0},{2,3},{3,2},{4,5},{5,4},{6,7},{7,6},{8,9},{9,8},{10,11... | collective-permute-start | bytes 3145736 | tf_op jit(solution)/shard_map/ppermute | solution.py:94
  107.0 20.5 %collective-permute-start.12 = (bf16[64,2048]{1,0:T(8,128)(2,1)S(1)}, bf16[64,2048]{1,0:T(8,128)(2,1)S(1)}, u32[]{:S(2)}, u32[]{:S(2)}) collective-permute-start(bf16[64,2048]{1,0:T(8,128)(2,1)S(1)} %get-tuple-element.18), channel_id=1, source_target_pairs={{0,4},{2,6},{4,0},{6,2},{1,5},{3,7},{5,1},{7,3},{8,12},{10,14},{12... | collective-permute-start | bytes 786440 | tf_op jit(solution)/shard_map/ppermute | solution.py:104
  107.8 19.8 %collective-permute-start.13 = (bf16[64,2048]{1,0:T(8,128)(2,1)S(1)}, bf16[64,2048]{1,0:T(8,128)(2,1)S(1)}, u32[]{:S(2)}, u32[]{:S(2)}) collective-permute-start(bf16[64,2048]{1,0:T(8,128)(2,1)S(1)} %get-tuple-element.18), channel_id=1, source_target_pairs={{0,6},{2,4},{4,2},{6,0},{1,7},{3,5},{5,3},{7,1},{8,14},{10,12},{12... | collective-permute-start | bytes 786440 | tf_op jit(solution)/shard_map/ppermute | solution.py:104
  109.4 18.1 %collective-permute-start.11 = (bf16[64,2048]{1,0:T(8,128)(2,1)S(1)}, bf16[64,2048]{1,0:T(8,128)(2,1)S(1)}, u32[]{:S(2)}, u32[]{:S(2)}) collective-permute-start(bf16[64,2048]{1,0:T(8,128)(2,1)S(1)} %get-tuple-element.18), channel_id=1, source_target_pairs={{0,2},{2,0},{4,6},{6,4},{1,3},{3,1},{5,7},{7,5},{8,10},{10,8},{12,... | collective-permute-start | bytes 786440 | tf_op jit(solution)/shard_map/ppermute | solution.py:104
  112.7 15.3 %collective-permute-start.4 = (f16[256,1792]{1,0:T(8,128)(2,1)S(1)}, f16[256,1792]{1,0:T(8,128)(2,1)S(1)}, u32[]{:S(2)}, u32[]{:S(2)}) collective-permute-start(f16[256,1792]{1,0:T(8,128)(2,1)S(1)} %fusion.26), channel_id=1, source_target_pairs={{0,8},{1,17},{8,0},{9,25},{16,24},{17,1},{24,16},{25,9},{2,10},{3,... | collective-permute-start | bytes 2752520 | tf_op jit(solution)/shard_map/ppermute | solution.py:68
  117.1 21.1 %collective-permute-start.6 = (f16[256,1792]{1,0:T(8,128)(2,1)S(1)}, f16[256,1792]{1,0:T(8,128)(2,1)S(1)}, u32[]{:S(2)}, u32[]{:S(2)}) collective-permute-start(f16[256,1792]{1,0:T(8,128)(2,1)S(1)} %fusion.27), channel_id=1, source_target_pairs={{0,8},{1,17},{8,0},{9,25},{16,24},{17,1},{24,16},{25,9},{2,10},{3,... | collective-permute-start | bytes 2752520 | tf_op jit(solution)/shard_map/ppermute | solution.py:68
  127.8 12.5 %collective-permute-start.14 = (bf16[4,64,2048]{2,1,0:T(8,128)(2,1)S(1)}, bf16[4,64,2048]{2,1,0:T(8,128)(2,1)S(1)}, u32[]{:S(2)}, u32[]{:S(2)}) collective-permute-start(bf16[4,64,2048]{2,1,0:T(8,128)(2,1)S(1)} %pad_maximum_fusion.12), channel_id=1, source_target_pairs={{0,1},{1,0},{2,3},{3,2},{4,5},{5,4},{6,7},{7,6},{8,9},{9,8},{10,11... | collective-permute-start | bytes 3145736 | tf_op jit(solution)/shard_map/ppermute | solution.py:94
  131.0 48.9 %collective-permute-start.5 = (f16[128,1792]{1,0:T(8,128)(2,1)}, f16[128,1792]{1,0:T(8,128)(2,1)S(1)}, u32[]{:S(2)}, u32[]{:S(2)}) collective-permute-start(f16[128,1792]{1,0:T(8,128)(2,1)} %multiply_convert_fusion.11), channel_id=1, source_target_pairs={{0,16},{1,9},{8,24},{9,1},{16,0},{17,25},{24,8},{25,17},{2,18},{3,... | collective-permute-start | bytes 1376264 | tf_op jit(solution)/shard_map/ppermute | solution.py:68
  141.0 19.1 %collective-permute-start.16 = (bf16[64,2048]{1,0:T(8,128)(2,1)S(1)}, bf16[64,2048]{1,0:T(8,128)(2,1)S(1)}, u32[]{:S(2)}, u32[]{:S(2)}) collective-permute-start(bf16[64,2048]{1,0:T(8,128)(2,1)S(1)} %get-tuple-element.19), channel_id=1, source_target_pairs={{0,4},{2,6},{4,0},{6,2},{1,5},{3,7},{5,1},{7,3},{8,12},{10,14},{12... | collective-permute-start | bytes 786440 | tf_op jit(solution)/shard_map/ppermute | solution.py:104
  141.1 19.0 %collective-permute-start.17 = (bf16[64,2048]{1,0:T(8,128)(2,1)S(1)}, bf16[64,2048]{1,0:T(8,128)(2,1)S(1)}, u32[]{:S(2)}, u32[]{:S(2)}) collective-permute-start(bf16[64,2048]{1,0:T(8,128)(2,1)S(1)} %get-tuple-element.19), channel_id=1, source_target_pairs={{0,6},{2,4},{4,2},{6,0},{1,7},{3,5},{5,3},{7,1},{8,14},{10,12},{12... | collective-permute-start | bytes 786440 | tf_op jit(solution)/shard_map/ppermute | solution.py:104
  143.7 15.5 %collective-permute-start.15 = (bf16[64,2048]{1,0:T(8,128)(2,1)S(1)}, bf16[64,2048]{1,0:T(8,128)(2,1)S(1)}, u32[]{:S(2)}, u32[]{:S(2)}) collective-permute-start(bf16[64,2048]{1,0:T(8,128)(2,1)S(1)} %get-tuple-element.19), channel_id=1, source_target_pairs={{0,2},{2,0},{4,6},{6,4},{1,3},{3,1},{5,7},{7,5},{8,10},{10,8},{12,... | collective-permute-start | bytes 786440 | tf_op jit(solution)/shard_map/ppermute | solution.py:104
  146.6 15.4 %collective-permute-start.26 = (f16[256,1792]{1,0:T(8,128)(2,1)S(1)}, f16[256,1792]{1,0:T(8,128)(2,1)S(1)}, u32[]{:S(2)}, u32[]{:S(2)}) collective-permute-start(f16[256,1792]{1,0:T(8,128)(2,1)S(1)} %fusion.30), channel_id=1, source_target_pairs={{0,8},{1,17},{8,0},{9,25},{16,24},{17,1},{24,16},{25,9},{2,10},{3,... | collective-permute-start | bytes 2752520 | tf_op jit(solution)/shard_map/ppermute | solution.py:68
  160.5 19.5 %collective-permute-start.7 = (f16[128,1792]{1,0:T(8,128)(2,1)S(1)}, f16[128,1792]{1,0:T(8,128)(2,1)S(1)}, u32[]{:S(2)}, u32[]{:S(2)}) collective-permute-start(f16[128,1792]{1,0:T(8,128)(2,1)S(1)} %multiply_convert_fusion.10), channel_id=1, source_target_pairs={{0,16},{1,9},{8,24},{9,1},{16,0},{17,25},{24,8},{25,17},{2,18},{3,... | collective-permute-start | bytes 1376264 | tf_op jit(solution)/shard_map/ppermute | solution.py:68
  165.3 15.5 %collective-permute-start.27 = (f16[128,1792]{1,0:T(8,128)(2,1)}, f16[128,1792]{1,0:T(8,128)(2,1)S(1)}, u32[]{:S(2)}, u32[]{:S(2)}) collective-permute-start(f16[128,1792]{1,0:T(8,128)(2,1)} %multiply_convert_fusion.5), channel_id=1, source_target_pairs={{0,16},{1,9},{8,24},{9,1},{16,0},{17,25},{24,8},{25,17},{2,18},{3,... | collective-permute-start | bytes 1376264 | tf_op jit(solution)/shard_map/ppermute | solution.py:68
  166.5 30.8 %collective-permute-start.34 = (bf16[64,2048]{1,0:T(8,128)(2,1)}, bf16[64,2048]{1,0:T(8,128)(2,1)S(1)}, u32[]{:S(2)}, u32[]{:S(2)}) collective-permute-start(bf16[64,2048]{1,0:T(8,128)(2,1)} %get-tuple-element.20), channel_id=1, source_target_pairs={{0,4},{2,6},{4,0},{6,2},{1,5},{3,7},{5,1},{7,3},{8,12},{10,14},{12... | collective-permute-start | bytes 786440 | tf_op jit(solution)/shard_map/ppermute | solution.py:104
  171.4 26.5 %collective-permute-start.35 = (bf16[64,2048]{1,0:T(8,128)(2,1)}, bf16[64,2048]{1,0:T(8,128)(2,1)}, u32[]{:S(2)}, u32[]{:S(2)}) collective-permute-start(bf16[64,2048]{1,0:T(8,128)(2,1)} %get-tuple-element.20), channel_id=1, source_target_pairs={{0,6},{2,4},{4,2},{6,0},{1,7},{3,5},{5,3},{7,1},{8,14},{10,12},{12... | collective-permute-start | bytes 786440 | tf_op jit(solution)/shard_map/ppermute | solution.py:104
  179.9 14.9 %collective-permute-start.33 = (bf16[64,2048]{1,0:T(8,128)(2,1)}, bf16[64,2048]{1,0:T(8,128)(2,1)S(1)}, u32[]{:S(2)}, u32[]{:S(2)}) collective-permute-start(bf16[64,2048]{1,0:T(8,128)(2,1)} %get-tuple-element.20), channel_id=1, source_target_pairs={{0,2},{2,0},{4,6},{6,4},{1,3},{3,1},{5,7},{7,5},{8,10},{10,8},{12,... | collective-permute-start | bytes 786440 | tf_op jit(solution)/shard_map/ppermute | solution.py:104
  180.0 37.9 %collective-permute-start.19 = (f16[256,1792]{1,0:T(8,128)(2,1)}, f16[256,1792]{1,0:T(8,128)(2,1)S(1)}, u32[]{:S(2)}, u32[]{:S(2)}) collective-permute-start(f16[256,1792]{1,0:T(8,128)(2,1)} %fusion.28), channel_id=1, source_target_pairs={{0,8},{1,17},{8,0},{9,25},{16,24},{17,1},{24,16},{25,9},{2,10},{3,... | collective-permute-start | bytes 2752520 | tf_op jit(solution)/shard_map/ppermute | solution.py:68
  180.8 41.6 %collective-permute-start.21 = (f16[256,1792]{1,0:T(8,128)(2,1)}, f16[256,1792]{1,0:T(8,128)(2,1)S(1)}, u32[]{:S(2)}, u32[]{:S(2)}) collective-permute-start(f16[256,1792]{1,0:T(8,128)(2,1)} %fusion.29), channel_id=1, source_target_pairs={{0,8},{1,17},{8,0},{9,25},{16,24},{17,1},{24,16},{25,9},{2,10},{3,... | collective-permute-start | bytes 2752520 | tf_op jit(solution)/shard_map/ppermute | solution.py:68
  197.3 14.4 %collective-permute-start.30 = (bf16[128,1792]{1,0:T(8,128)(2,1)S(1)}, bf16[128,1792]{1,0:T(8,128)(2,1)S(1)}, u32[]{:S(2)}, u32[]{:S(2)}) collective-permute-start(bf16[128,1792]{1,0:T(8,128)(2,1)S(1)} %get-tuple-element.40), channel_id=1, source_target_pairs={{0,16},{1,9},{8,24},{9,1},{16,0},{17,25},{24,8},{25,17},{2,18},{3,... | collective-permute-start | bytes 1376264 | tf_op jit(solution)/shard_map/ppermute | solution.py:68
  197.9 19.0 %collective-permute-start.28 = (bf16[128,1792]{1,0:T(8,128)(2,1)S(1)}, bf16[128,1792]{1,0:T(8,128)(2,1)S(1)}, u32[]{:S(2)}, u32[]{:S(2)}) collective-permute-start(bf16[128,1792]{1,0:T(8,128)(2,1)S(1)} %get-tuple-element.41), channel_id=1, source_target_pairs={{0,16},{1,9},{8,24},{9,1},{16,0},{17,25},{24,8},{25,17},{2,18},{3,... | collective-permute-start | bytes 1376264 | tf_op jit(solution)/shard_map/ppermute | solution.py:68
  206.8 22.2 %collective-permute-start.36 = (bf16[4,64,2048]{2,1,0:T(8,128)(2,1)S(1)}, bf16[4,64,2048]{2,1,0:T(8,128)(2,1)S(1)}, u32[]{:S(2)}, u32[]{:S(2)}) collective-permute-start(bf16[4,64,2048]{2,1,0:T(8,128)(2,1)S(1)} %pad_maximum_fusion.14), channel_id=1, source_target_pairs={{0,1},{1,0},{2,3},{3,2},{4,5},{5,4},{6,7},{7,6},{8,9},{9,8},{10,11... | collective-permute-start | bytes 3145736 | tf_op jit(solution)/shard_map/ppermute | solution.py:94
  211.7 73.8 %collective-permute-start.9 = (bf16[256,1792]{1,0:T(8,128)(2,1)}, bf16[256,1792]{1,0:T(8,128)(2,1)}, u32[]{:S(2)}, u32[]{:S(2)}) collective-permute-start(bf16[256,1792]{1,0:T(8,128)(2,1)} %pad_maximum_fusion.17), channel_id=1, source_target_pairs={{0,8},{1,17},{8,0},{9,25},{16,24},{17,1},{24,16},{25,9},{2,10},{3,... | collective-permute-start | bytes 2752520 | tf_op jit(solution)/shard_map/ppermute | solution.py:68
  217.0 29.1 %collective-permute-start.31 = (bf16[256,1792]{1,0:T(8,128)(2,1)S(1)}, bf16[256,1792]{1,0:T(8,128)(2,1)S(1)}, u32[]{:S(2)}, u32[]{:S(2)}) collective-permute-start(bf16[256,1792]{1,0:T(8,128)(2,1)S(1)} %pad_maximum_fusion.20), channel_id=1, source_target_pairs={{0,8},{1,17},{8,0},{9,25},{16,24},{17,1},{24,16},{25,9},{2,10},{3,... | collective-permute-start | bytes 2752520 | tf_op jit(solution)/shard_map/ppermute | solution.py:68
  217.9 39.8 %collective-permute-start.29 = (bf16[256,1792]{1,0:T(8,128)(2,1)S(1)}, bf16[256,1792]{1,0:T(8,128)(2,1)}, u32[]{:S(2)}, u32[]{:S(2)}) collective-permute-start(bf16[256,1792]{1,0:T(8,128)(2,1)S(1)} %pad_maximum_fusion.19), channel_id=1, source_target_pairs={{0,8},{1,17},{8,0},{9,25},{16,24},{17,1},{24,16},{25,9},{2,10},{3,... | collective-permute-start | bytes 2752520 | tf_op jit(solution)/shard_map/ppermute | solution.py:68
  223.3 55.4 %collective-permute-start.20 = (f16[128,1792]{1,0:T(8,128)(2,1)}, f16[128,1792]{1,0:T(8,128)(2,1)S(1)}, u32[]{:S(2)}, u32[]{:S(2)}) collective-permute-start(f16[128,1792]{1,0:T(8,128)(2,1)} %multiply_convert_fusion.8), channel_id=1, source_target_pairs={{0,16},{1,9},{8,24},{9,1},{16,0},{17,25},{24,8},{25,17},{2,18},{3,... | collective-permute-start | bytes 1376264 | tf_op jit(solution)/shard_map/ppermute | solution.py:68
  229.1 49.6 %collective-permute-start.22 = (f16[128,1792]{1,0:T(8,128)(2,1)}, f16[128,1792]{1,0:T(8,128)(2,1)}, u32[]{:S(2)}, u32[]{:S(2)}) collective-permute-start(f16[128,1792]{1,0:T(8,128)(2,1)} %multiply_convert_fusion.7), channel_id=1, source_target_pairs={{0,16},{1,9},{8,24},{9,1},{16,0},{17,25},{24,8},{25,17},{2,18},{3,... | collective-permute-start | bytes 1376264 | tf_op jit(solution)/shard_map/ppermute | solution.py:68
  246.1 24.3 %collective-permute-start.37 = (f16[256,1792]{1,0:T(8,128)(2,1)}, f16[256,1792]{1,0:T(8,128)(2,1)}, u32[]{:S(2)}, u32[]{:S(2)}) collective-permute-start(f16[256,1792]{1,0:T(8,128)(2,1)} %fusion.31), channel_id=1, source_target_pairs={{0,8},{1,17},{8,0},{9,25},{16,24},{17,1},{24,16},{25,9},{2,10},{3,... | collective-permute-start | bytes 2752520 | tf_op jit(solution)/shard_map/ppermute | solution.py:68
  270.4 42.0 %collective-permute-start.32 = (f32[256,2048]{1,0:T(8,128)}, f32[256,2048]{1,0:T(8,128)}, u32[]{:S(2)}, u32[]{:S(2)}) collective-permute-start(f32[256,2048]{1,0:T(8,128)} %convolution_add_fusion.2), channel_id=1, source_target_pairs={{0,1},{1,0},{2,3},{3,2},{4,5},{5,4},{6,7},{7,6},{8,9},{9,8},{10,11... | collective-permute-start | bytes 6291464 | tf_op jit(solution)/shard_map/ppermute | solution.py:94
  287.2 13.5 %collective-permute-start.41 = (bf16[128,1792]{1,0:T(8,128)(2,1)S(1)}, bf16[128,1792]{1,0:T(8,128)(2,1)S(1)}, u32[]{:S(2)}, u32[]{:S(2)}) collective-permute-start(bf16[128,1792]{1,0:T(8,128)(2,1)S(1)} %get-tuple-element.37), channel_id=1, source_target_pairs={{0,16},{1,9},{8,24},{9,1},{16,0},{17,25},{24,8},{25,17},{2,18},{3,... | collective-permute-start | bytes 1376264 | tf_op jit(solution)/shard_map/ppermute | solution.py:68
  287.8 22.7 %collective-permute-start.39 = (bf16[128,1792]{1,0:T(8,128)(2,1)S(1)}, bf16[128,1792]{1,0:T(8,128)(2,1)S(1)}, u32[]{:S(2)}, u32[]{:S(2)}) collective-permute-start(bf16[128,1792]{1,0:T(8,128)(2,1)S(1)} %get-tuple-element.38), channel_id=1, source_target_pairs={{0,16},{1,9},{8,24},{9,1},{16,0},{17,25},{24,8},{25,17},{2,18},{3,... | collective-permute-start | bytes 1376264 | tf_op jit(solution)/shard_map/ppermute | solution.py:68
  292.7 31.0 %collective-permute-start.24 = (bf16[256,1792]{1,0:T(8,128)(2,1)S(1)}, bf16[256,1792]{1,0:T(8,128)(2,1)}, u32[]{:S(2)}, u32[]{:S(2)}) collective-permute-start(bf16[256,1792]{1,0:T(8,128)(2,1)S(1)} %pad_maximum_fusion.18), channel_id=1, source_target_pairs={{0,8},{1,17},{8,0},{9,25},{16,24},{17,1},{24,16},{25,9},{2,10},{3,... | collective-permute-start | bytes 2752520 | tf_op jit(solution)/shard_map/ppermute | solution.py:68
  301.8 33.6 %collective-permute-start.42 = (bf16[256,1792]{1,0:T(8,128)(2,1)}, bf16[256,1792]{1,0:T(8,128)(2,1)}, u32[]{:S(2)}, u32[]{:S(2)}) collective-permute-start(bf16[256,1792]{1,0:T(8,128)(2,1)} %pad_maximum_fusion.22), channel_id=1, source_target_pairs={{0,8},{1,17},{8,0},{9,25},{16,24},{17,1},{24,16},{25,9},{2,10},{3,... | collective-permute-start | bytes 2752520 | tf_op jit(solution)/shard_map/ppermute | solution.py:68
  311.6 25.4 %collective-permute-start.40 = (bf16[256,1792]{1,0:T(8,128)(2,1)}, bf16[256,1792]{1,0:T(8,128)(2,1)}, u32[]{:S(2)}, u32[]{:S(2)}) collective-permute-start(bf16[256,1792]{1,0:T(8,128)(2,1)} %pad_maximum_fusion.21), channel_id=1, source_target_pairs={{0,8},{1,17},{8,0},{9,25},{16,24},{17,1},{24,16},{25,9},{2,10},{3,... | collective-permute-start | bytes 2752520 | tf_op jit(solution)/shard_map/ppermute | solution.py:68
  331.4 42.2 %collective-permute-start.10 = (f32[256,2048]{1,0:T(8,128)}, f32[256,2048]{1,0:T(8,128)}, u32[]{:S(2)}, u32[]{:S(2)}) collective-permute-start(f32[256,2048]{1,0:T(8,128)} %fusion.97), channel_id=1, source_target_pairs={{0,1},{1,0},{2,3},{3,2},{4,5},{5,4},{6,7},{7,6},{8,9},{9,8},{10,11... | collective-permute-start | bytes 6291464 | tf_op jit(solution)/shard_map/ppermute | solution.py:94
  334.9 43.5 %collective-permute-start.25 = (f32[256,2048]{1,0:T(8,128)}, f32[256,2048]{1,0:T(8,128)}, u32[]{:S(2)}, u32[]{:S(2)}) collective-permute-start(f32[256,2048]{1,0:T(8,128)} %fusion.98), channel_id=1, source_target_pairs={{0,1},{1,0},{2,3},{3,2},{4,5},{5,4},{6,7},{7,6},{8,9},{9,8},{10,11... | collective-permute-start | bytes 6291464 | tf_op jit(solution)/shard_map/ppermute | solution.py:94
  350.3 33.4 %collective-permute-start.43 = (f32[256,2048]{1,0:T(8,128)}, f32[256,2048]{1,0:T(8,128)}, u32[]{:S(2)}, u32[]{:S(2)}) collective-permute-start(f32[256,2048]{1,0:T(8,128)} %convolution_add_fusion), channel_id=1, source_target_pairs={{0,1},{1,0},{2,3},{3,2},{4,5},{5,4},{6,7},{7,6},{8,9},{9,8},{10,11... | collective-permute-start | bytes 6291464 | tf_op jit(solution)/shard_map/ppermute | solution.py:94
  392.0 19.9 %collective-permute-start.44 = (bf16[128,2048]{1,0:T(8,128)(2,1)S(1)}, bf16[128,2048]{1,0:T(8,128)(2,1)}, u32[]{:S(2)}, u32[]{:S(2)}) collective-permute-start(bf16[128,2048]{1,0:T(8,128)(2,1)S(1)} %bitcast.240), channel_id=1, source_target_pairs={{0,2},{2,0},{4,6},{6,4},{1,3},{3,1},{5,7},{7,5},{8,10},{10,8},{12,... | collective-permute-start | bytes 1572872 | tf_op jit(solution)/shard_map/ppermute | solution.py:150
  394.0 24.2 %collective-permute-start.45 = (bf16[128,2048]{1,0:T(8,128)(2,1)}, bf16[128,2048]{1,0:T(8,128)(2,1)}, u32[]{:S(2)}, u32[]{:S(2)}) collective-permute-start(bf16[128,2048]{1,0:T(8,128)(2,1)} %bitcast.47), channel_id=1, source_target_pairs={{0,2},{2,0},{4,6},{6,4},{1,3},{3,1},{5,7},{7,5},{8,10},{10,8},{12,... | collective-permute-start | bytes 1572872 | tf_op jit(solution)/shard_map/ppermute | solution.py:150
  394.0 35.2 %collective-permute-start.46 = (bf16[128,2048]{1,0:T(8,128)(2,1)}, bf16[128,2048]{1,0:T(8,128)(2,1)S(1)}, u32[]{:S(2)}, u32[]{:S(2)}) collective-permute-start(bf16[128,2048]{1,0:T(8,128)(2,1)} %bitcast.57), channel_id=1, source_target_pairs={{0,2},{2,0},{4,6},{6,4},{1,3},{3,1},{5,7},{7,5},{8,10},{10,8},{12,... | collective-permute-start | bytes 1572872 | tf_op jit(solution)/shard_map/ppermute | solution.py:150
  396.0 44.4 %collective-permute-start.47 = (bf16[128,2048]{1,0:T(8,128)(2,1)}, bf16[128,2048]{1,0:T(8,128)(2,1)}, u32[]{:S(2)}, u32[]{:S(2)}) collective-permute-start(bf16[128,2048]{1,0:T(8,128)(2,1)} %bitcast.72), channel_id=1, source_target_pairs={{0,2},{2,0},{4,6},{6,4},{1,3},{3,1},{5,7},{7,5},{8,10},{10,8},{12,... | collective-permute-start | bytes 1572872 | tf_op jit(solution)/shard_map/ppermute | solution.py:150
  443.3 32.9 %collective-permute-start.49 = (bf16[64,2048]{1,0:T(8,128)(2,1)}, bf16[64,2048]{1,0:T(8,128)(2,1)}, u32[]{:S(2)}, u32[]{:S(2)}) collective-permute-start(bf16[64,2048]{1,0:T(8,128)(2,1)} %fusion.68), channel_id=1, source_target_pairs={{0,4},{2,6},{4,0},{6,2},{1,5},{3,7},{5,1},{7,3},{8,12},{10,14},{12... | collective-permute-start | bytes 786440 | tf_op jit(solution)/shard_map/ppermute | solution.py:150
  445.4 36.4 %collective-permute-start.48 = (bf16[64,2048]{1,0:T(8,128)(2,1)}, bf16[64,2048]{1,0:T(8,128)(2,1)}, u32[]{:S(2)}, u32[]{:S(2)}) collective-permute-start(bf16[64,2048]{1,0:T(8,128)(2,1)} %fusion.67), channel_id=1, source_target_pairs={{0,4},{2,6},{4,0},{6,2},{1,5},{3,7},{5,1},{7,3},{8,12},{10,14},{12... | collective-permute-start | bytes 786440 | tf_op jit(solution)/shard_map/ppermute | solution.py:150
  446.2 41.2 %collective-permute-start.51 = (bf16[64,2048]{1,0:T(8,128)(2,1)}, bf16[64,2048]{1,0:T(8,128)(2,1)}, u32[]{:S(2)}, u32[]{:S(2)}) collective-permute-start(bf16[64,2048]{1,0:T(8,128)(2,1)} %fusion.70), channel_id=1, source_target_pairs={{0,4},{2,6},{4,0},{6,2},{1,5},{3,7},{5,1},{7,3},{8,12},{10,14},{12... | collective-permute-start | bytes 786440 | tf_op jit(solution)/shard_map/ppermute | solution.py:150
  448.3 43.5 %collective-permute-start.50 = (bf16[64,2048]{1,0:T(8,128)(2,1)}, bf16[64,2048]{1,0:T(8,128)(2,1)S(1)}, u32[]{:S(2)}, u32[]{:S(2)}) collective-permute-start(bf16[64,2048]{1,0:T(8,128)(2,1)} %fusion.69), channel_id=1, source_target_pairs={{0,4},{2,6},{4,0},{6,2},{1,5},{3,7},{5,1},{7,3},{8,12},{10,14},{12... | collective-permute-start | bytes 786440 | tf_op jit(solution)/shard_map/ppermute | solution.py:150
  (76 other events, 823.1 us)
